TPU v7x, 512 devices: a whole 4x8x8 slice. The times are simulated.
512 devices in a mesh: section: 16 (over y, core), tensor: 8 (over z), dp: 4 (over x).
Axes of the slice: x: 4, y: 8, z: 8, core: 2. Of those that a mesh axis runs over, the one named last changes fastest.
Arguments:
- section_out: bfloat16 [16, 512, 12288], P('section', 'dp', 'tensor'), may hold values from -6 to 6
- embedded: bfloat16 [512, 12288], P('dp', 'tensor'), may hold values from -6 to 6
- section_grad: bfloat16 [16, 512, 12288], P('section', 'dp', 'tensor'), may hold values from -0.26367188 to 0.26367188
- loss_grad: bfloat16 [512, 12288], P('dp', 'tensor'), may hold values from -0.26367188 to 0.26367188
- assign: int32 [16, 96, 1], P('section', 'tensor'), may hold values from 0 to 15; in each aligned block of 12 rows (0 to 11, 12 to 23, ..., all dimensions but the last counted through in order) at most 2 rows name the same one
- state_a: bfloat16 [16, 256, 128, 128], P('section', 'tensor'), may hold values from -6 to 54, as said below
- state_g: bfloat16 [16, 256, 128, 128], P('section', 'tensor'), may hold values from -6 to 54, as said below
Outputs:
- update: float32 [16, 96, 128, 128], P('section', 'tensor')
Inputs may be any that keep to these rules, and one draw needn't show every extreme that they name: `assign`: within the rows of one device (aligned blocks of 12 rows along the first two dimensions), no section is named more than 2 times, a bound that some block reaches. `state_a`: each block is symmetric. `state_g`: each block is symmetric.
All inputs are finite; a program needn't handle non-finite values. Where the computation divides by a largest or mean magnitude, that divisor is 1e-20 or more.
Results may differ from a plain program's by a relative error of at most 0.0003.
Values may be sent and summed in bfloat16 or wider, within the bound.
No kernel may reach another device: no remote copies, remote signals or barrier semaphores. Data moves between devices by JAX's collectives and lax.ppermute only.
A program may use at most 64 MiB of HBM per device.

v0:
```python
import jax
import jax.numpy as jnp
from jax import lax
from jax.sharding import PartitionSpec as P

BLK = 128
NS_ITERS = 5


HIGH = lax.Precision.HIGHEST


def shifted(shard, axis, by):
    length = lax.axis_size(axis)
    pairs = [(i, i + by) for i in range(length) if 0 <= i + by < length]
    return lax.ppermute(shard, axis, pairs)


def newton_inverse(matrix):
    extent = matrix.shape[-1]
    identity = jnp.eye(extent, dtype=matrix.dtype)
    row_bound = jnp.max(jnp.sum(jnp.abs(matrix), axis=-1), axis=-1)
    approx = identity / row_bound[..., None, None]
    for repeat in range(NS_ITERS):
        product = jnp.matmul(matrix, approx, precision=HIGH)
        approx = jnp.matmul(approx, 2.0 * identity - product, precision=HIGH)
    return approx


def precondition(held_a, held_g, batch_a, batch_g, gradient):
    identity = jnp.eye(batch_a.shape[-1], dtype=jnp.float32)
    matrix_a = 0.5 * held_a.astype(jnp.float32) + 0.5 * batch_a + 0.1 * identity
    matrix_g = 0.5 * held_g.astype(jnp.float32) + 0.5 * batch_g + 0.1 * identity
    inv_a = newton_inverse(matrix_a)
    inv_g = newton_inverse(matrix_g)
    return jnp.matmul(jnp.matmul(inv_a, gradient, precision=HIGH), inv_g, precision=HIGH)


def token_sums(part_a, part_g, part_w):
    return lax.psum((part_a, part_g, part_w), "dp")


def body(section_out, embedded, section_grad, loss_grad, assign, state_a, state_g):
    section_idx = lax.axis_index("section")
    section_count = lax.axis_size("section")
    arrived = shifted(section_out[0], "section", 1)
    returned = shifted(section_grad[0], "section", -1)
    inputs = jnp.where(section_idx == 0, embedded, arrived)
    out_grad = jnp.where(section_idx == section_count - 1, loss_grad, returned)
    tokens, feature_width = inputs.shape
    total_tokens = tokens * lax.axis_size("dp")
    block_count = feature_width // BLK
    in_blocks = inputs.reshape(tokens, block_count, BLK)
    grad_blocks = out_grad.reshape(tokens, block_count, BLK)
    part_a = jnp.einsum("tnb,tnc->nbc", in_blocks, in_blocks, preferred_element_type=jnp.float32)
    part_g = jnp.einsum(
        "tnb,tnc->nbc", grad_blocks, grad_blocks, preferred_element_type=jnp.float32
    )
    part_w = jnp.einsum("tnb,tnc->nbc", in_blocks, grad_blocks, preferred_element_type=jnp.float32)
    target = assign[0, :, 0]
    block_order = jnp.arange(block_count, dtype=jnp.int32)
    same_dest = (target[:, None] == target[None, :]) & (block_order[None, :] < block_order[:, None])
    rank_in = jnp.sum(same_dest.astype(jnp.int32), axis=1)
    slot_total = state_a.shape[1]
    capacity = slot_total // section_count
    slot_index = target * capacity + rank_in
    sum_a, sum_g, sum_w = token_sums(part_a, part_g, part_w)
    batch_a = sum_a / total_tokens

    def place_slots(blocks):
        filled = jnp.zeros((slot_total, BLK, BLK), jnp.float32).at[slot_index].set(blocks)
        return filled.reshape(section_count, capacity, BLK, BLK)

    got_a, got_g, got_w = (
        lax.all_to_all(place_slots(batch_a), "section", split_axis=0, concat_axis=0, tiled=True),
        lax.all_to_all(place_slots(sum_g), "section", split_axis=0, concat_axis=0, tiled=True),
        lax.all_to_all(place_slots(sum_w), "section", split_axis=0, concat_axis=0, tiled=True),
    )
    result = precondition(
        state_a[0],
        state_g[0],
        got_a.reshape(slot_total, BLK, BLK),
        got_g.reshape(slot_total, BLK, BLK),
        got_w.reshape(slot_total, BLK, BLK),
    )
    returned_updates = lax.all_to_all(
        result.reshape(section_count, capacity, BLK, BLK),
        "section",
        split_axis=0,
        concat_axis=0,
        tiled=True,
    )
    update = returned_updates.reshape(slot_total, BLK, BLK)[slot_index]
    return update[None]


def solution(mesh):
    in_specs = (
        P("section", "dp", "tensor"),
        P("dp", "tensor"),
        P("section", "dp", "tensor"),
        P("dp", "tensor"),
        P("section", "tensor", None),
        P("section", "tensor", None, None),
        P("section", "tensor", None, None),
    )
    out_specs = P("section", "tensor", None, None)
    return jax.shard_map(body, mesh=mesh, in_specs=in_specs, out_specs=out_specs, check_vma=False)
```

profile of v0, /device:TPU:1, one launch (start us, length us, event | category | flops | bytes accessed | tf_op | source)
XLA Modules:
  0.0 350.0 jit_solution(1637301912167964897)
XLA Ops:
  6.5 1.3 copy.35
  7.8 8.8 %collective-permute-start.1 = (bf16[128,1536]{0,1:T(8,128)(2,1)S(1)}, bf16[128,1536]{0,1:T(8,128)(2,1)S(1)}, u32[]{:S(2)}, u32[]{:S(2)}) collective-permute-start(bf16[128,1536]{0,1:T(8,128)(2,1)S(1)} %bitcast.91), channel_id=1, source_target_pairs={{32,0},{64,32},{96,64},{128,96},{160,128},{192,160},{224,192},{256... | collective-permute-start | bytes 1179656 | tf_op jit(solution)/shard_map/ppermute | solution.py:16
  16.6 1.2 copy.30
  17.8 1.9 collective-permute-start
  19.8 1.2 copy.31
  21.3 1.3 fusion.60
  22.6 1.9 collective-permute-done
  24.5 1.3 fusion.58
  25.8 1.3 fusion.53
  27.3 76.3 %all-reduce.3.cloned.1.call-done = (f32[12,128,128]{2,1,0:T(8,128)}, f32[12,128,128]{2,1,0:T(8,128)}, f32[12,128,128]{2,1,0:T(8,128)}) async-done(((f32[12,128,128]{2,1,0:T(8,128)}, f32[12,128,128]{2,1,0:T(8,128)}, f32[12,128,128]{2,1,0:T(8,128)}), (f32[12,128,128]{2,1,0:T(8,128)}, f32[12,128,128]{2,1,0:T(8,128)}, f32[12,128,128]{2,1,0:T(8,128)})) %all-reduce.3.cloned.1.call-update) | async-done | bytes 2359312 | tf_op jit(solution)/shard_map/psum | solution.py:40
  103.6 1.2 broadcast_multiply_fusion
  106.1 1.3 copy-done
  107.4 7.4 %all-to-all-start = ((f32[16,2,128,128]{3,2,1,0:T(8,128)}), f32[16,2,128,128]{3,2,1,0:T(8,128)S(1)}, u32[]{:S(2)}, u32[]{:S(2)}) async-start(f32[16,2,128,128]{3,2,1,0:T(8,128)} %bitcast.80), calls=%async_computation | async-start | bytes 4194304 | tf_op jit(solution)/shard_map/all_to_all | solution.py:75
  114.9 1.5 broadcast.71.clone
  116.4 2.8 scatter_fusion.2
  119.2 44.6 %all-to-all-done = f32[16,2,128,128]{3,2,1,0:T(8,128)S(1)} async-done(((f32[16,2,128,128]{3,2,1,0:T(8,128)}), f32[16,2,128,128]{3,2,1,0:T(8,128)S(1)}, u32[]{:S(2)}, u32[]{:S(2)}) %all-to-all-start) | async-done | bytes 2097184 | tf_op jit(solution)/shard_map/all_to_all | solution.py:75
  163.8 5.0 %all-to-all-start.2 = ((f32[16,2,128,128]{3,2,1,0:T(8,128)}), f32[16,2,128,128]{3,2,1,0:T(8,128)}, u32[]{:S(2)}, u32[]{:S(2)}) async-start(f32[16,2,128,128]{3,2,1,0:T(8,128)} %bitcast.81), calls=%async_computation.2 | async-start | bytes 4194304 | tf_op jit(solution)/shard_map/all_to_all | solution.py:76
  168.8 1.6 broadcast.71.clone.2
  170.4 2.9 scatter_fusion.1
  173.3 44.5 %all-to-all-done.2 = f32[16,2,128,128]{3,2,1,0:T(8,128)} async-done(((f32[16,2,128,128]{3,2,1,0:T(8,128)}), f32[16,2,128,128]{3,2,1,0:T(8,128)}, u32[]{:S(2)}, u32[]{:S(2)}) %all-to-all-start.2) | async-done | bytes 2097184 | tf_op jit(solution)/shard_map/all_to_all | solution.py:76
  217.8 5.3 %all-to-all-start.1 = ((f32[16,2,128,128]{3,2,1,0:T(8,128)}), f32[16,2,128,128]{3,2,1,0:T(8,128)}, u32[]{:S(2)}, u32[]{:S(2)}) async-start(f32[16,2,128,128]{3,2,1,0:T(8,128)} %bitcast.79), calls=%async_computation.1 | async-start | bytes 4194304 | tf_op jit(solution)/shard_map/all_to_all | solution.py:77
  223.1 3.0 abs_reduce_fusion
  226.5 2.6 fusion.1
  229.1 2.3 fusion.25
  231.4 2.4 fusion.12
  233.7 2.3 fusion.61
  236.1 2.3 fusion.10
  238.3 2.5 fusion.62
  240.8 2.3 fusion.8
  243.1 2.3 fusion.63
  245.4 2.3 fusion.6
  247.7 2.3 fusion.28
  250.0 2.8 fusion.22
  252.8 2.3 fusion.64
  255.1 2.3 fusion.54
  257.4 2.3 fusion.20
  259.6 2.3 fusion.55
  261.9 2.5 fusion.18
  264.4 2.3 fusion.56
  266.7 2.3 fusion.16
  269.0 2.3 fusion.57
  271.3 2.2 fusion.4
  273.5 3.8 %fusion.14 = f32[32,128,128]{2,1,0:T(8,128)} fusion(f32[32,128,128]{2,1,0:T(8,128)S(1)} %fusion.16, f32[32,128,128]{2,1,0:T(8,128)S(1)} %fusion.57, f32[128,128]{1,0:T(8,128)S(1)} %fusion.48), kind=kOutput, calls=%fused_computation.21 | convolution fusion | flops 805830656 | bytes 6356992 | tf_op jit(solution)/shard_map/dot_general | solution.py:26
  277.3 4.4 %fusion.59 = f32[32,128,128]{2,1,0:T(8,128)S(1)} fusion(f32[32,128,128]{2,1,0:T(8,128)} %fusion.14, f32[32,128,128]{2,1,0:T(8,128)} %bitcast.13), kind=kOutput, calls=%fused_computation.76 | convolution fusion | flops 805306368 | bytes 6291456 | tf_op jit(solution)/shard_map/dot_general | solution.py:36
  281.7 3.5 %fusion.65 = f32[32,128,128]{2,1,0:T(8,128)} fusion(f32[32,128,128]{2,1,0:T(8,128)S(1)} %fusion.59, f32[32,128,128]{2,1,0:T(8,128)S(1)} %fusion.4), kind=kOutput, calls=%fused_computation.82 | convolution fusion | flops 805306368 | bytes 6291456 | tf_op jit(solution)/shard_map/dot_general | solution.py:36
  285.3 7.2 %all-to-all-start.3 = ((f32[16,2,128,128]{3,2,1,0:T(8,128)}), f32[16,2,128,128]{3,2,1,0:T(8,128)S(1)}, u32[]{:S(2)}, u32[]{:S(2)}) async-start(f32[16,2,128,128]{3,2,1,0:T(8,128)} %bitcast.82), calls=%async_computation.3 | async-start | bytes 4194304 | tf_op jit(solution)/shard_map/all_to_all | solution.py:86
  292.5 48.9 %all-to-all-done.3 = f32[16,2,128,128]{3,2,1,0:T(8,128)S(1)} async-done(((f32[16,2,128,128]{3,2,1,0:T(8,128)}), f32[16,2,128,128]{3,2,1,0:T(8,128)S(1)}, u32[]{:S(2)}, u32[]{:S(2)}) %all-to-all-start.3) | async-done | bytes 2097184 | tf_op jit(solution)/shard_map/all_to_all | solution.py:86
  341.4 1.5 gather_fusion
  (30 shorter events, 2.2 us)
Async XLA Ops:
  6.5 14.5 %copy-start.4 = (bf16[128,1536]{1,0:T(8,128)(2,1)S(1)}, bf16[128,1536]{1,0:T(8,128)(2,1)}, u32[]{:S(2)}) copy-start(bf16[128,1536]{1,0:T(8,128)(2,1)} %param.10) | copy-start | bytes 1179652
  6.5 97.1 %all-reduce.3.cloned.1.call-start = ((), (), s32[]{:S(2)}) async-start(), calls=%async_computation.4 | async-start | bytes 4718592 | tf_op jit(solution)/shard_map/psum | solution.py:40
  7.8 13.4 %collective-permute-start.1 = (bf16[128,1536]{0,1:T(8,128)(2,1)S(1)}, bf16[128,1536]{0,1:T(8,128)(2,1)S(1)}, u32[]{:S(2)}, u32[]{:S(2)}) collective-permute-start(bf16[128,1536]{0,1:T(8,128)(2,1)S(1)} %bitcast.91), channel_id=1, source_target_pairs={{32,0},{64,32},{96,64},{128,96},{160,128},{192,160},{224,192},{256... | collective-permute-start | bytes 1179656 | tf_op jit(solution)/shard_map/ppermute | solution.py:16
  17.8 6.6 %collective-permute-start = (bf16[128,1536]{0,1:T(8,128)(2,1)S(1)}, bf16[128,1536]{0,1:T(8,128)(2,1)S(1)}, u32[]{:S(2)}, u32[]{:S(2)}) collective-permute-start(bf16[128,1536]{0,1:T(8,128)(2,1)S(1)} %bitcast.90), channel_id=1, source_target_pairs={{0,32},{32,64},{64,96},{96,128},{128,160},{160,192},{192,224},{224... | collective-permute-start | bytes 1179656 | tf_op jit(solution)/shard_map/ppermute | solution.py:16
  25.8 1.3 copy-start.5
  106.1 1.4 copy-start
  107.4 56.4 %all-to-all-start = ((f32[16,2,128,128]{3,2,1,0:T(8,128)}), f32[16,2,128,128]{3,2,1,0:T(8,128)S(1)}, u32[]{:S(2)}, u32[]{:S(2)}) async-start(f32[16,2,128,128]{3,2,1,0:T(8,128)} %bitcast.80), calls=%async_computation | async-start | bytes 4194304 | tf_op jit(solution)/shard_map/all_to_all | solution.py:75
  114.8 1.5 copy-start.3
  163.8 54.0 %all-to-all-start.2 = ((f32[16,2,128,128]{3,2,1,0:T(8,128)}), f32[16,2,128,128]{3,2,1,0:T(8,128)}, u32[]{:S(2)}, u32[]{:S(2)}) async-start(f32[16,2,128,128]{3,2,1,0:T(8,128)} %bitcast.81), calls=%async_computation.2 | async-start | bytes 4194304 | tf_op jit(solution)/shard_map/all_to_all | solution.py:76
  168.8 1.6 copy-start.2
  217.8 5.3 %copy-start.1 = (bf16[1,32,128,128]{3,2,1,0:T(8,128)(2,1)S(1)}, bf16[1,32,128,128]{3,2,1,0:T(8,128)(2,1)}, u32[]{:S(2)}) copy-start(bf16[1,32,128,128]{3,2,1,0:T(8,128)(2,1)} %param.13) | copy-start | bytes 3145732
  217.8 59.5 %all-to-all-start.1 = ((f32[16,2,128,128]{3,2,1,0:T(8,128)}), f32[16,2,128,128]{3,2,1,0:T(8,128)}, u32[]{:S(2)}, u32[]{:S(2)}) async-start(f32[16,2,128,128]{3,2,1,0:T(8,128)} %bitcast.79), calls=%async_computation.1 | async-start | bytes 4194304 | tf_op jit(solution)/shard_map/all_to_all | solution.py:77
  285.3 56.2 %all-to-all-start.3 = ((f32[16,2,128,128]{3,2,1,0:T(8,128)}), f32[16,2,128,128]{3,2,1,0:T(8,128)S(1)}, u32[]{:S(2)}, u32[]{:S(2)}) async-start(f32[16,2,128,128]{3,2,1,0:T(8,128)} %bitcast.82), calls=%async_computation.3 | async-start | bytes 4194304 | tf_op jit(solution)/shard_map/all_to_all | solution.py:86
Sparse Core Ops, SparseCore 0:
  27.2 76.3 all-reduce.2
where the time goes:
time: 354 us; the launch traced here: 350 us
  waiting for transfers between devices  216 us (61%)
  matrix products  59.8 us (17%)
  starting transfers between devices  35.6 us (10%)
  local copies, waits for them, and re-layouts  17.1 us (5%)
  between operations  14 us (4%)
  other arithmetic  7.29 us (2%)
    psum x1, waiting for transfers between devices, token_sums(): return lax.psum((part_a, part_g, part_w), 'dp')  76.3 us
    all_to_all x1, waiting for transfers between devices, body(): lax.all_to_all(result.reshape(section_count, capacity, BLK, BLK), 'sectio...  48.9 us
    all_to_all x1, waiting for transfers between devices, body(): lax.all_to_all(place_slots(batch_a), 'section', split_axis=0, concat_axis...  44.6 us
    all_to_all x1, waiting for transfers between devices, body(): lax.all_to_all(place_slots(sum_g), 'section', split_axis=0, concat_axis=0...  44.5 us
    dot_general x10, matrix products, newton_inverse(): approx = jnp.matmul(approx, 2.0 * identity - product, precision=HIGH)  25 us
    dot_general x10, matrix products, newton_inverse(): product = jnp.matmul(matrix, approx, precision=HIGH)  23.1 us
    ppermute x2, starting transfers between devices, shifted(): return lax.ppermute(shard, axis, pairs)  10.7 us
    all_to_all x1, starting transfers between devices, body(): lax.all_to_all(place_slots(batch_a), 'section', split_axis=0, concat_axis...  7.43 us
  transfers between devices with their start and end apart: 7, of which 5 were waited for; matrix products, arithmetic and copies ran while one was open for 19% of the time, Pallas kernels for 0%

commit v1 on v0

v1 whole, which is shorter than its diff:
```python
import functools

import jax
import jax.numpy as jnp
from jax import lax
from jax.experimental import pallas as pl
from jax.experimental.pallas import tpu as pltpu
from jax.sharding import PartitionSpec as P

BLK = 128
NS_ITERS = 5
DAMPING = 0.1
DP = 4


def pack_state_kernel(part_ref, a_ref, g_ref, out_ref):
    out_ref[:, 0] = a_ref[...]
    out_ref[:, 1] = g_ref[...]


def pack_state(state_a, state_g, part):
    slots = state_a.shape[0]
    rows = BLK // DP
    block = pl.BlockSpec((slots, rows, BLK), lambda i, part: (0, part[0], 0))
    return pl.pallas_call(
        pack_state_kernel,
        out_shape=jax.ShapeDtypeStruct((slots, 2, rows, BLK), state_a.dtype),
        grid_spec=pltpu.PrefetchScalarGridSpec(
            num_scalar_prefetch=1,
            grid=(1,),
            in_specs=[block, block],
            out_specs=pl.BlockSpec((slots, 2, rows, BLK), lambda i, part: (0, 0, 0, 0)),
        ),
        name="pack_state",
    )(part, state_a, state_g)


def pack_tokens_kernel(section_ref, out_ref, embedded_ref, grad_ref, loss_ref, in_send, grad_send):
    width = in_send.shape[2]
    section = section_ref[0]
    last = section_ref[1]

    @pl.when(section == last)
    def _():
        for part in range(DP):
            in_send[part] = embedded_ref[:, part * width:(part + 1) * width]

    @pl.when(section != last)
    def _():
        for part in range(DP):
            in_send[part] = out_ref[:, part * width:(part + 1) * width]

    @pl.when(section == 0)
    def _():
        for part in range(DP):
            grad_send[part] = loss_ref[:, part * width:(part + 1) * width]

    @pl.when(section != 0)
    def _():
        for part in range(DP):
            grad_send[part] = grad_ref[:, part * width:(part + 1) * width]


def pack_tokens(place, section_out, embedded, section_grad, loss_grad):
    tokens, features = section_out.shape
    shape = jax.ShapeDtypeStruct((DP, tokens, features // DP), section_out.dtype)
    vmem = pl.BlockSpec(memory_space=pltpu.VMEM)
    return pl.pallas_call(
        pack_tokens_kernel,
        out_shape=(shape, shape),
        in_specs=[pl.BlockSpec(memory_space=pltpu.SMEM)] + [vmem] * 4,
        out_specs=(vmem, vmem),
        name="pack_tokens",
    )(place, section_out, embedded, section_grad, loss_grad)


def select_kernel(assign_ref, got_ref, out_ref):
    count = out_ref.shape[0]
    holders = [assign_ref[j] for j in range(count)]
    for j in range(count):
        rank = jnp.int32(0)
        for earlier in range(j):
            rank = rank + (holders[earlier] == holders[j]).astype(jnp.int32)
        out_ref[j] = got_ref[holders[j] * 2 + rank]


def select(assign, got):
    vmem = pl.BlockSpec(memory_space=pltpu.VMEM)
    return pl.pallas_call(
        select_kernel,
        out_shape=jax.ShapeDtypeStruct((assign.shape[0],) + got.shape[1:], got.dtype),
        in_specs=[pl.BlockSpec(memory_space=pltpu.SMEM), vmem],
        out_specs=vmem,
        name="select",
    )(assign, got)


def halves(value):
    high = value.astype(jnp.bfloat16)
    low = (value - high.astype(jnp.float32)).astype(jnp.bfloat16)
    return high, low


def product(left, right):
    lhs = jnp.concatenate([left[0], left[0], left[1]], axis=1)
    rhs = jnp.concatenate([right[0], right[1], right[0]], axis=0)
    return jnp.dot(lhs, rhs, preferred_element_type=jnp.float32)


def precondition_kernel(tokens_total, x_ref, held_ref, out_ref):
    count = out_ref.shape[0]
    chunks, _, tokens, _ = x_ref.shape
    row = lax.broadcasted_iota(jnp.int32, (BLK, BLK), 0)
    column = lax.broadcasted_iota(jnp.int32, (BLK, BLK), 1)
    identity = (row == column).astype(jnp.float32)

    def start(matrix):
        bound = jnp.max(jnp.sum(jnp.abs(matrix), axis=0, keepdims=True), axis=1, keepdims=True)
        return identity - matrix / bound, bound

    rest_a, rest_g, value, bound_g = [], [], [], []
    for j in range(count):
        columns = slice(j * BLK, (j + 1) * BLK)
        both = jnp.concatenate(
            [
                x_ref[:, 0, :, columns].reshape(chunks * tokens, BLK),
                x_ref[:, 1, :, columns].reshape(chunks * tokens, BLK),
            ],
            axis=1,
        )
        sums = lax.dot_general(both, both, (((0,), (0,)), ((), ())), preferred_element_type=jnp.float32)
        held_a = held_ref[:, j, 0].reshape(BLK, BLK).astype(jnp.float32)
        held_g = held_ref[:, j, 1].reshape(BLK, BLK).astype(jnp.float32)
        batch_a = sums[:BLK, :BLK] / tokens_total
        matrix_a = 0.5 * held_a + 0.5 * batch_a + DAMPING * identity
        matrix_g = 0.5 * held_g + 0.5 * sums[BLK:, BLK:] + DAMPING * identity
        left, bound_a = start(matrix_a)
        right, bound = start(matrix_g)
        rest_a.append(left)
        rest_g.append(right)
        value.append(sums[:BLK, BLK:] / bound_a)
        bound_g.append(bound)
    for step in range(NS_ITERS):
        for j in range(count):
            left, right, middle = halves(rest_a[j]), halves(rest_g[j]), halves(value[j])
            if step < NS_ITERS - 1:
                rhs = [jnp.concatenate([l, m], axis=1) for l, m in zip(left, middle)]
                both = product(left, rhs)
                rest_a[j] = both[:, :BLK]
                value[j] = value[j] + both[:, BLK:]
                middle = halves(value[j])
                lhs = [jnp.concatenate([r, m], axis=0) for r, m in zip(right, middle)]
                both = product(lhs, right)
                rest_g[j] = both[:BLK]
                value[j] = value[j] + both[BLK:]
            else:
                value[j] = value[j] + product(left, middle)
                value[j] = value[j] + product(halves(value[j]), right)
    for j in range(count):
        out_ref[j] = value[j] / bound_g[j]


def precondition(x, held, tokens_total):
    count = held.shape[1]
    vmem = pl.BlockSpec(memory_space=pltpu.VMEM)
    return pl.pallas_call(
        functools.partial(precondition_kernel, tokens_total),
        out_shape=jax.ShapeDtypeStruct((count, BLK, BLK), jnp.float32),
        in_specs=[vmem, vmem],
        out_specs=vmem,
        compiler_params=pltpu.CompilerParams(vmem_limit_bytes=32 * 1024 * 1024),
        name="precondition",
    )(x, held)


def spread(array, axis):
    return lax.all_to_all(array, axis, split_axis=0, concat_axis=0, tiled=True)


def body(section_out, embedded, section_grad, loss_grad, assign, state_a, state_g):
    section = lax.axis_index("section")
    sections = lax.axis_size("section")
    part = lax.axis_index("dp")
    slots = state_a.shape[1]
    blocks = assign.shape[1]
    tokens, features = embedded.shape
    rows = BLK // DP

    packed = pack_state(state_a[0], state_g[0], part.astype(jnp.int32).reshape(1))
    got = spread(packed.reshape(sections, slots // sections * 2 * rows, BLK), "section")

    place = jnp.stack([section, jnp.full_like(section, sections - 1)]).astype(jnp.int32)
    in_send, grad_send = pack_tokens(place, section_out[0], embedded, section_grad[0], loss_grad)
    inputs = lax.ppermute(in_send, "section", [(i, (i + 1) % sections) for i in range(sections)])
    grads = lax.ppermute(grad_send, "section", [(i, (i - 1) % sections) for i in range(sections)])
    x = spread(jnp.stack([inputs, grads], axis=1), "dp")

    mine = select(assign[0, :, 0], got.reshape(slots, 2 * rows, BLK))
    held = spread(mine.reshape(DP, blocks // DP * 2 * rows, BLK), "dp")
    result = precondition(x, held.reshape(DP, blocks // DP, 2, rows, BLK), tokens * DP)
    return lax.all_gather(result, "dp", axis=0, tiled=True)[None]


def solution(mesh):
    in_specs = (
        P("section", "dp", "tensor"),
        P("dp", "tensor"),
        P("section", "dp", "tensor"),
        P("dp", "tensor"),
        P("section", "tensor", None),
        P("section", "tensor", None, None),
        P("section", "tensor", None, None),
    )
    out_specs = P("section", "tensor", None, None)
    return jax.shard_map(body, mesh=mesh, in_specs=in_specs, out_specs=out_specs, check_vma=False)
```

time: 354 us -> 75.8 us (0.21)
  the two profiles are of different devices: /device:TPU:1 before, /device:TPU:448 now
where the time goes in v1:
time: 75.8 us; the launch traced here: 74.4 us
  blocking collectives  23.7 us (31%)
  waiting for transfers between devices  23.4 us (31%)
  starting transfers between devices  14.5 us (19%)
  Pallas kernels  9.45 us (12%)
  local copies, waits for them, and re-layouts  1.67 us (2%)
  other arithmetic  1.63 us (2%)
    all_gather x1, blocking collectives, body(): return lax.all_gather(result, 'dp', axis=0, tiled=True)[None]  14 us
    ppermute x1, waiting for transfers between devices, body(): lax.ppermute(in_send, 'section', [(i, (i + 1) % sections) for i in range(...  13.8 us
    all_to_all x2, starting transfers between devices, spread(): return lax.all_to_all(array, axis, split_axis=0, concat_axis=0, tiled=True)  11.5 us
    all_to_all x1, blocking collectives, spread(): return lax.all_to_all(array, axis, split_axis=0, concat_axis=0, tiled=True)  9.66 us
    all_to_all x2, waiting for transfers between devices, spread(): return lax.all_to_all(array, axis, split_axis=0, concat_axis=0, tiled=True)  9.59 us
    pallas_call x1, Pallas kernels, precondition(): pl.pallas_call(functools.partial(precondition_kernel, tokens_total), out_...  3.45 us
    ppermute x1, starting transfers between devices, body(): lax.ppermute(grad_send, 'section', [(i, (i - 1) % sections) for i in rang...  2.55 us
    pallas_call x1, Pallas kernels, pack_tokens(): pl.pallas_call(pack_tokens_kernel, out_shape=(shape, shape), in_specs=[pl...  2.33 us
  transfers between devices with their start and end apart: 4, of which 2 were waited for; matrix products, arithmetic and copies ran while one was open for 2% of the time, Pallas kernels for 6%

profile of v1, /device:TPU:448, one launch (start us, length us, event | category | flops | bytes accessed | tf_op | source)
XLA Modules:
  0.0 74.4 jit_solution(7107062172918446554)
XLA Ops:
  0.0 1.9 %pack_state.1 = bf16[32,2,32,128]{3,2,1,0:T(8,128)(2,1)} custom-call(s32[1]{0:T(128)} %bitcast.6.part_ref, bf16[32,128,128]{2,1,0:T(8,128)(2,1)} %bitcast.18, bf16[32,128,128]{2,1,0:T(8,128)(2,1)} %bitcast.19), custom_call_target="tpu_custom_call" | custom-call | tf_op jit(solution)/shard_map/pack_state/pallas_call | solution.py:25
  1.9 7.2 %all-to-all-start.1 = ((bf16[16,128,128]{2,1,0:T(8,128)(2,1)}), bf16[16,128,128]{2,1,0:T(8,128)(2,1)S(1)}, u32[]{:S(2)}, u32[]{:S(2)}) async-start(bf16[16,128,128]{2,1,0:T(8,128)(2,1)} %bitcast.17), calls=%async_computation.1 | async-start | bytes 1048576 | tf_op jit(solution)/shard_map/all_to_all | solution.py:177
  9.1 0.7 pad_add_fusion.section_ref
  9.7 2.3 %pack_tokens.1 = (bf16[4,128,384]{2,1,0:T(8,128)(2,1)}, bf16[4,128,384]{2,1,0:T(8,128)(2,1)}) custom-call(s32[2]{0:T(128)} %pad_add_fusion.section_ref, bf16[128,1536]{1,0:T(8,128)(2,1)} %bitcast.21, bf16[128,1536]{1,0:T(8,128)(2,1)} %embedded_ref.1, bf16[128,1536]{1,0:T(8,128)(2,1)} %bitcast.22, bf16[128,1536]{1,0:T(8,128)(2,1)} %loss_ref.1), custom_call_target="tpu_custom_call" | custom-call | tf_op jit(solution)/shard_map/pack_tokens/pallas_call | solution.py:68
  12.1 0.4 collective-permute-start
  12.5 2.6 %collective-permute-start.1 = (bf16[4,128,384]{2,1,0:T(8,128)(2,1)}, bf16[4,128,384]{2,1,0:T(8,128)(2,1)S(1)}, u32[]{:S(2)}, u32[]{:S(2)}) collective-permute-start(bf16[4,128,384]{2,1,0:T(8,128)(2,1)} %get-tuple-element.8), channel_id=1, source_target_pairs={{0,480},{32,0},{64,32},{96,64},{128,96},{160,128},{192,160},{224,1... | collective-permute-start | bytes 1179656 | tf_op jit(solution)/shard_map/ppermute | solution.py:195
  15.0 13.8 %collective-permute-done = bf16[4,128,384]{2,1,0:T(8,128)(2,1)S(1)} collective-permute-done((bf16[4,128,384]{2,1,0:T(8,128)(2,1)}, bf16[4,128,384]{2,1,0:T(8,128)(2,1)S(1)}, u32[]{:S(2)}, u32[]{:S(2)}) %collective-permute-start) | collective-permute-done | bytes 393248 | tf_op jit(solution)/shard_map/ppermute | solution.py:194
  28.9 0.0 collective-permute-done.1
  28.9 1.0 %pad_maximum_fusion = bf16[4,2,128,384]{3,2,1,0:T(8,128)(2,1)} fusion(bf16[4,1,128,384]{3,2,1,0:T(8,128)(2,1)S(1)} %bitcast.24, bf16[4,1,128,384]{3,2,1,0:T(8,128)(2,1)S(1)} %bitcast.23), kind=kLoop, calls=%fused_computation | loop fusion | flops 393216 | bytes 1572864 | tf_op jit(solution)/shard_map/stack | solution.py:196
  29.8 0.0 all-to-all-done.1
  29.8 0.0 copy-start
  29.8 0.8 %copy-done = bf16[16,128,128]{2,1,0:T(8,128)(2,1)} copy-done((bf16[16,128,128]{2,1,0:T(8,128)(2,1)}, bf16[16,128,128]{2,1,0:T(8,128)(2,1)S(1)}, u32[]{:S(2)}) %copy-start) | copy-done | bytes 524312
  30.6 4.3 %all-to-all-start = ((bf16[4,2,128,384]{3,2,1,0:T(8,128)(2,1)}), bf16[4,2,128,384]{3,2,1,0:T(8,128)(2,1)S(1)}, u32[]{:S(2)}, u32[]{:S(2)}) async-start(bf16[4,2,128,384]{3,2,1,0:T(8,128)(2,1)} %pad_maximum_fusion), calls=%async_computation | async-start | bytes 1572864 | tf_op jit(solution)/shard_map/all_to_all | solution.py:177
  34.9 1.8 %select.1 = bf16[12,64,128]{2,1,0:T(8,128)(2,1)} custom-call(s32[12]{0:T(128)} %bitcast.25, bf16[32,64,128]{2,1,0:T(8,128)(2,1)} %bitcast.16), custom_call_target="tpu_custom_call" | custom-call | tf_op jit(solution)/shard_map/select/pallas_call | solution.py:89
  36.7 9.6 %all-to-all-done.x_ref = bf16[4,2,128,384]{3,2,1,0:T(8,128)(2,1)S(1)} async-done(((bf16[4,2,128,384]{3,2,1,0:T(8,128)(2,1)}), bf16[4,2,128,384]{3,2,1,0:T(8,128)(2,1)S(1)}, u32[]{:S(2)}, u32[]{:S(2)}) %all-to-all-start) | async-done | bytes 786464 | tf_op jit(solution)/shard_map/all_to_all | solution.py:177
  46.3 9.7 %all_to_all.15 = bf16[4,192,128]{2,1,0:T(8,128)(2,1)S(1)} all-to-all(bf16[4,192,128]{2,1,0:T(8,128)(2,1)} %bitcast.20), channel_id=1, replica_groups=mesh['section'=16,'tensor'=8,'dp'=4] {'dp'}, dimensions={0} | all-to-all | bytes 393216 | tf_op jit(solution)/shard_map/all_to_all | solution.py:177
  56.0 3.5 %precondition.1 = f32[3,128,128]{2,1,0:T(8,128)S(1)} custom-call(bf16[4,2,128,384]{3,2,1,0:T(8,128)(2,1)S(1)} %all-to-all-done.x_ref, bf16[4,3,2,32,128]{4,3,2,1,0:T(8,128)(2,1)S(1)} %bitcast.14), custom_call_target="tpu_custom_call" | custom-call | tf_op jit(solution)/shard_map/precondition/pallas_call | solution.py:166
  59.4 14.0 %all_gather.3 = f32[12,128,128]{2,1,0:T(8,128)S(1)} all-gather(f32[3,128,128]{2,1,0:T(8,128)S(1)} %precondition.1), channel_id=1, replica_groups=mesh['section'=16,'tensor'=8,'dp'=4] {'dp'}, dimensions={0}, use_global_device_ids=true | all-gather | bytes 983040 | tf_op jit(solution)/shard_map/all_gather | solution.py:201
  73.5 0.9 %copy.9 = f32[1,12,128,128]{3,2,1,0:T(8,128)} copy(f32[1,12,128,128]{3,2,1,0:T(8,128)S(1)} %bitcast.15) | data formatting | bytes 1572864
Async XLA Ops:
  1.9 28.0 %all-to-all-start.1 = ((bf16[16,128,128]{2,1,0:T(8,128)(2,1)}), bf16[16,128,128]{2,1,0:T(8,128)(2,1)S(1)}, u32[]{:S(2)}, u32[]{:S(2)}) async-start(bf16[16,128,128]{2,1,0:T(8,128)(2,1)} %bitcast.17), calls=%async_computation.1 | async-start | bytes 1048576 | tf_op jit(solution)/shard_map/all_to_all | solution.py:177
  12.1 16.8 %collective-permute-start = (bf16[4,128,384]{2,1,0:T(8,128)(2,1)}, bf16[4,128,384]{2,1,0:T(8,128)(2,1)S(1)}, u32[]{:S(2)}, u32[]{:S(2)}) collective-permute-start(bf16[4,128,384]{2,1,0:T(8,128)(2,1)} %get-tuple-element.7), channel_id=1, source_target_pairs={{0,32},{32,64},{64,96},{96,128},{128,160},{160,192},{192,224},{224... | collective-permute-start | bytes 1179656 | tf_op jit(solution)/shard_map/ppermute | solution.py:194
  12.5 16.4 %collective-permute-start.1 = (bf16[4,128,384]{2,1,0:T(8,128)(2,1)}, bf16[4,128,384]{2,1,0:T(8,128)(2,1)S(1)}, u32[]{:S(2)}, u32[]{:S(2)}) collective-permute-start(bf16[4,128,384]{2,1,0:T(8,128)(2,1)} %get-tuple-element.8), channel_id=1, source_target_pairs={{0,480},{32,0},{64,32},{96,64},{128,96},{160,128},{192,160},{224,1... | collective-permute-start | bytes 1179656 | tf_op jit(solution)/shard_map/ppermute | solution.py:195
  29.8 0.8 %copy-start = (bf16[16,128,128]{2,1,0:T(8,128)(2,1)}, bf16[16,128,128]{2,1,0:T(8,128)(2,1)S(1)}, u32[]{:S(2)}) copy-start(bf16[16,128,128]{2,1,0:T(8,128)(2,1)S(1)} %all-to-all-done.1) | copy-start | bytes 1572868
  30.6 15.7 %all-to-all-start = ((bf16[4,2,128,384]{3,2,1,0:T(8,128)(2,1)}), bf16[4,2,128,384]{3,2,1,0:T(8,128)(2,1)S(1)}, u32[]{:S(2)}, u32[]{:S(2)}) async-start(bf16[4,2,128,384]{3,2,1,0:T(8,128)(2,1)} %pad_maximum_fusion), calls=%async_computation | async-start | bytes 1572864 | tf_op jit(solution)/shard_map/all_to_all | solution.py:177

commit v2 on v1

v2 whole, which is shorter than its diff:
```python
import functools

import jax
import jax.numpy as jnp
from jax import lax
from jax.experimental import pallas as pl
from jax.experimental.pallas import tpu as pltpu
from jax.sharding import PartitionSpec as P

BLK = 128
NS_ITERS = 5
DAMPING = 0.1
DP = 4
PIECES = 4


SMALL = pltpu.CompilerParams(vmem_limit_bytes=4 * 1024 * 1024)
ANY = pl.BlockSpec(memory_space=pl.ANY)
VMEM = pl.BlockSpec(memory_space=pltpu.VMEM)
SMEM = pl.BlockSpec(memory_space=pltpu.SMEM)


def run(copies, sems):
    made = [pltpu.make_async_copy(source, target, sems.at[i]) for i, (source, target) in enumerate(copies)]
    for copy in made:
        copy.start()
    for copy in made:
        copy.wait()


def pack_state_kernel(a_ref, g_ref, out_ref, sems):
    slots, _, rows, _ = out_ref.shape
    mine = pl.ds(pl.multiple_of(lax.axis_index("dp") * rows, rows), rows)
    copies = []
    for first in range(0, slots, slots // PIECES):
        piece = pl.ds(first, slots // PIECES)
        copies.append((a_ref.at[piece, mine, :], out_ref.at[piece, 0]))
        copies.append((g_ref.at[piece, mine, :], out_ref.at[piece, 1]))
    run(copies, sems)


def pack_state(state_a, state_g):
    state_a = pltpu.with_memory_space_constraint(state_a, pltpu.HBM)
    state_g = pltpu.with_memory_space_constraint(state_g, pltpu.HBM)
    return pl.pallas_call(
        pack_state_kernel,
        out_shape=pltpu.VMEM((state_a.shape[0], 2, BLK // DP, BLK), state_a.dtype),
        in_specs=[ANY, ANY],
        out_specs=VMEM,
        scratch_shapes=[pltpu.SemaphoreType.DMA((2 * PIECES,))],
        compiler_params=SMALL,
        name="pack_state",
    )(state_a, state_g)


def pack_tokens_kernel(assign_ref, arrived_ref, embedded_ref, returned_ref, loss_ref, *refs):
    send_refs, slot_ref, sems = refs[:-2], refs[-2], refs[-1]
    for j in range(assign_ref.shape[0]):
        rank = jnp.int32(0)
        for earlier in range(j):
            rank = rank + (assign_ref[earlier] == assign_ref[j]).astype(jnp.int32)
        slot_ref[j] = assign_ref[j] * 2 + rank
    width = send_refs[0].shape[2]
    section, part = lax.axis_index("section"), lax.axis_index("dp")
    last_section = lax.axis_size("section") - 1

    for first in (True, False):
        for last in (True, False):
            if first and last:
                continue

            @pl.when(((section == 0) == first) & ((section == last_section) == last))
            def _():
                copies = []
                for which, source in enumerate((embedded_ref if first else arrived_ref, loss_ref if last else returned_ref)):
                    for turn in range(DP):
                        start = pl.multiple_of(lax.rem(part + turn, DP) * width, width)
                        copies.append((source.at[:, pl.ds(start, width)], send_refs[turn].at[which]))
                run(copies, sems)


def pack_tokens(assign, arrived, embedded, returned, loss_grad):
    tokens, features = arrived.shape
    shape = jax.ShapeDtypeStruct((2, tokens, features // DP), arrived.dtype)
    return pl.pallas_call(
        pack_tokens_kernel,
        out_shape=(shape,) * DP + (pltpu.SMEM(assign.shape, jnp.int32),),
        in_specs=[SMEM] + [ANY] * 4,
        out_specs=(ANY,) * DP + (SMEM,),
        scratch_shapes=[pltpu.SemaphoreType.DMA((2 * DP,))],
        compiler_params=SMALL,
        cost_estimate=pl.CostEstimate(flops=15 * 10**9, bytes_accessed=2**20, transcendentals=0),
        name="pack_tokens",
    )(assign, arrived, embedded, returned, loss_grad)


def select_kernel(slot_ref, got_ref, out_ref):
    for j in range(out_ref.shape[0]):
        out_ref[j] = got_ref[slot_ref[j]]


def select(slot, got):
    return pl.pallas_call(
        select_kernel,
        out_shape=jax.ShapeDtypeStruct((slot.shape[0],) + got.shape[1:], got.dtype),
        in_specs=[SMEM, VMEM],
        out_specs=VMEM,
        compiler_params=SMALL,
        name="select",
    )(slot, got)


def halves(value):
    high = value.astype(jnp.bfloat16)
    low = (value - high.astype(jnp.float32)).astype(jnp.bfloat16)
    return high, low


def product(left, right):
    lhs = jnp.concatenate([left[0], left[0], left[1]], axis=1)
    rhs = jnp.concatenate([right[0], right[1], right[0]], axis=0)
    return jnp.dot(lhs, rhs, preferred_element_type=jnp.float32)


def gram_kernel(*refs):
    chunk_refs, out_ref = refs[:-1], refs[-1]
    for j in range(out_ref.shape[0]):
        columns = slice(j * BLK, (j + 1) * BLK)
        inputs = jnp.concatenate([ref[0, :, columns] for ref in chunk_refs], axis=0)
        grads = jnp.concatenate([ref[1, :, columns] for ref in chunk_refs], axis=0)
        both = jnp.concatenate([inputs, grads], axis=1)
        out_ref[j] = lax.dot_general(both, both, (((0,), (0,)), ((), ())), preferred_element_type=jnp.float32)


def gram(chunks):
    return pl.pallas_call(
        gram_kernel,
        out_shape=jax.ShapeDtypeStruct((chunks[0].shape[2] // BLK, 2 * BLK, 2 * BLK), jnp.float32),
        in_specs=[VMEM] * DP,
        out_specs=VMEM,
        compiler_params=pltpu.CompilerParams(vmem_limit_bytes=8 * 1024 * 1024),
        cost_estimate=pl.CostEstimate(flops=10**9, bytes_accessed=2**20, transcendentals=0),
        name="gram",
    )(*chunks)


def precondition_kernel(tokens_total, sums_ref, held_ref, out_ref):
    count = out_ref.shape[0]
    row = lax.broadcasted_iota(jnp.int32, (BLK, BLK), 0)
    column = lax.broadcasted_iota(jnp.int32, (BLK, BLK), 1)
    identity = (row == column).astype(jnp.float32)

    def start(matrix):
        bound = jnp.max(jnp.sum(jnp.abs(matrix), axis=0, keepdims=True), axis=1, keepdims=True)
        return identity - matrix / bound, bound

    rest_a, rest_g, value, bound_g = [], [], [], []
    for j in range(count):
        held_a = held_ref[:, j, 0].reshape(BLK, BLK).astype(jnp.float32)
        held_g = held_ref[:, j, 1].reshape(BLK, BLK).astype(jnp.float32)
        batch_a = sums_ref[j, :BLK, :BLK] / tokens_total
        batch_g = sums_ref[j, BLK:, BLK:]
        left, bound_a = start(0.5 * held_a + 0.5 * batch_a + DAMPING * identity)
        right, bound = start(0.5 * held_g + 0.5 * batch_g + DAMPING * identity)
        rest_a.append(left)
        rest_g.append(right)
        value.append(sums_ref[j, :BLK, BLK:] / bound_a)
        bound_g.append(bound)
    for step in range(NS_ITERS):
        for j in range(count):
            left, right, middle = halves(rest_a[j]), halves(rest_g[j]), halves(value[j])
            if step < NS_ITERS - 1:
                rhs = [jnp.concatenate([l, m], axis=1) for l, m in zip(left, middle)]
                both = product(left, rhs)
                rest_a[j] = both[:, :BLK]
                value[j] = value[j] + both[:, BLK:]
                middle = halves(value[j])
                lhs = [jnp.concatenate([r, m], axis=0) for r, m in zip(right, middle)]
                both = product(lhs, right)
                rest_g[j] = both[:BLK]
                value[j] = value[j] + both[BLK:]
            else:
                value[j] = value[j] + product(left, middle)
                value[j] = value[j] + product(halves(value[j]), right)
    for j in range(count):
        out_ref[j] = value[j] / bound_g[j]


def precondition(sums, held, tokens_total):
    return pl.pallas_call(
        functools.partial(precondition_kernel, tokens_total),
        out_shape=jax.ShapeDtypeStruct((held.shape[1], BLK, BLK), jnp.float32),
        in_specs=[VMEM, VMEM],
        out_specs=VMEM,
        compiler_params=pltpu.CompilerParams(vmem_limit_bytes=8 * 1024 * 1024),
        name="precondition",
    )(sums, held)


def spread(array, axis):
    return lax.all_to_all(array, axis, split_axis=0, concat_axis=0, tiled=True)


def hop(array, axis, by):
    size = lax.axis_size(axis)
    return lax.ppermute(array, axis, [(i, (i + by) % size) for i in range(size)])


def body(section_out, embedded, section_grad, loss_grad, assign, state_a, state_g):
    sections = lax.axis_size("section")
    slots = state_a.shape[1]
    blocks = assign.shape[1]
    tokens, features = embedded.shape
    rows = BLK // DP

    arrived = hop(section_out[0], "section", 1)
    packed, section_grad = lax.optimization_barrier((pack_state(state_a[0], state_g[0]), section_grad))
    returned = hop(section_grad[0], "section", -1)
    got = spread(packed.reshape(sections, slots // sections * 2 * rows, BLK), "section")

    *sends, slot = pack_tokens(assign[0, :, 0], arrived, embedded, returned, loss_grad)
    chunks = [sends[0]] + [hop(sends[turn], "dp", turn) for turn in range(1, DP)]

    mine = select(slot, got.reshape(slots, 2 * rows, BLK))
    held = spread(mine.reshape(DP, blocks // DP * 2 * rows, BLK), "dp")
    held = held.reshape(DP, blocks // DP, 2, rows, BLK)

    result = precondition(gram(chunks), held, tokens * DP)
    return lax.all_gather(result, "dp", axis=0, tiled=True)[None]


def solution(mesh):
    in_specs = (
        P("section", "dp", "tensor"),
        P("dp", "tensor"),
        P("section", "dp", "tensor"),
        P("dp", "tensor"),
        P("section", "tensor", None),
        P("section", "tensor", None, None),
        P("section", "tensor", None, None),
    )
    out_specs = P("section", "tensor", None, None)
    return jax.shard_map(body, mesh=mesh, in_specs=in_specs, out_specs=out_specs, check_vma=False)
```

time: 75.8 us -> 59.2 us (0.78); the launches traced: 74.4 us -> 58.8 us
  waiting for transfers between devices: 23.4 us -> 9.71 us
  starting transfers between devices: 14.5 us -> 26 us
  blocking collectives: 23.7 us -> 14.4 us
  Pallas kernels: 9.45 us -> 7.03 us
  other arithmetic: 1.63 us -> 0 us
    ppermute x2 -> x5, waiting for transfers between devices: 13.8 us -> 0.01 us  [hop(): lax.ppermute(array, axis, [(i, (i + by) % size) for i in range(size)])]
    ppermute x2 -> x5, starting transfers between devices: 2.96 us -> 14.3 us  [hop(): lax.ppermute(array, axis, [(i, (i + by) % size) for i in range(size)])]
    all_to_all x1 -> x0, blocking collectives: 9.66 us -> none  [spread(): return lax.all_to_all(array, axis, split_axis=0, concat_axis=0, tiled=True)]
    pallas_call x3 -> x4, Pallas kernels: 6 us -> 3.92 us  [the longest x1 1.98 us: pack_state(): pl.pallas_call(pack_state_kernel, out_shape=pltpu.VMEM((state_a.shape[0],...]
    another operation x2 -> x0, other arithmetic: 1.63 us -> none  [the longest x1 0.97 us: body(): x = spread(jnp.stack([inputs, grads], axis=1), 'dp')]
    unnamed x3 -> x9, local copies, waits for them, and re-layouts: 1.67 us -> 1.5 us
  transfers between devices with their start and end apart: 4 -> 7, of which waited for: 2 -> 2; matrix products, arithmetic and copies ran while one was open for 2% -> 0% of each run, Pallas kernels for 6% -> 7%
where the time goes in v2:
time: 59.2 us; the launch traced here: 58.8 us
  starting transfers between devices  26 us (44%)
  blocking collectives  14.4 us (24%)
  waiting for transfers between devices  9.71 us (16%)
  Pallas kernels  7.03 us (12%)
  local copies, waits for them, and re-layouts  1.5 us (3%)
    all_gather x1, blocking collectives, body(): return lax.all_gather(result, 'dp', axis=0, tiled=True)[None]  14.4 us
    ppermute x5, starting transfers between devices, hop(): lax.ppermute(array, axis, [(i, (i + by) % size) for i in range(size)])  14.3 us
    all_to_all x2, starting transfers between devices, spread(): return lax.all_to_all(array, axis, split_axis=0, concat_axis=0, tiled=True)  11.7 us
    all_to_all x2, waiting for transfers between devices, spread(): return lax.all_to_all(array, axis, split_axis=0, concat_axis=0, tiled=True)  9.69 us
    pallas_call x1, Pallas kernels, precondition(): pl.pallas_call(functools.partial(precondition_kernel, tokens_total), out_...  3.11 us
    pallas_call x1, Pallas kernels, pack_state(): pl.pallas_call(pack_state_kernel, out_shape=pltpu.VMEM((state_a.shape[0],...  1.98 us
    unnamed x9, local copies, waits for them, and re-layouts  1.5 us
  transfers between devices with their start and end apart: 7, of which 2 were waited for; matrix products, arithmetic and copies ran while one was open for 0% of the time, Pallas kernels for 7%

profile of v2, /device:TPU:448, one launch (start us, length us, event | category | flops | bytes accessed | tf_op | source)
XLA Modules:
  0.0 58.8 jit_solution(16811728760763794435)
XLA Ops:
  0.0 0.0 collective-permute-start
  0.0 0.0 copy-start.3
  0.0 2.0 %pack_state.1 = bf16[32,2,32,128]{3,2,1,0:T(8,128)(2,1)} custom-call(bf16[32,128,128]{2,1,0:T(8,128)(2,1)} %bitcast.14, bf16[32,128,128]{2,1,0:T(8,128)(2,1)} %bitcast.15), custom_call_target="tpu_custom_call" | custom-call | tf_op jit(solution)/shard_map/pack_state/pallas_call | solution.py:45
  2.0 0.0 copy-done.3
  2.0 3.0 %collective-permute-start.1 = (bf16[128,1536]{1,0:T(8,128)(2,1)S(1)}, bf16[128,1536]{1,0:T(8,128)(2,1)S(1)}, u32[]{:S(2)}, u32[]{:S(2)}) collective-permute-start(bf16[128,1536]{1,0:T(8,128)(2,1)S(1)} %bitcast.17), channel_id=1, source_target_pairs={{0,480},{32,0},{64,32},{96,64},{128,96},{160,128},{192,160},{224,1... | collective-permute-start | bytes 1179656 | tf_op jit(solution)/shard_map/ppermute | solution.py:206
  5.0 0.0 copy-start
  5.0 0.0 copy-start.1
  5.0 7.4 %all-to-all-start = ((bf16[16,128,128]{2,1,0:T(8,128)(2,1)}), bf16[16,128,128]{2,1,0:T(8,128)(2,1)S(1)}, u32[]{:S(2)}, u32[]{:S(2)}) async-start(bf16[16,128,128]{2,1,0:T(8,128)(2,1)} %bitcast.5), calls=%async_computation | async-start | bytes 1048576 | tf_op jit(solution)/shard_map/all_to_all | solution.py:201
  12.4 0.0 copy-start.2
  12.4 0.0 collective-permute-done.arrived_ref
  12.4 0.0 collective-permute-done.1.returned_ref
  12.4 0.0 copy-done
  12.4 0.0 copy-done.1
  12.4 0.6 %copy-done.2 = s32[1,12,1]{1,2,0:T(1,128)S(1)} copy-done((s32[1,12,1]{1,2,0:T(1,128)S(1)}, s32[1,12,1]{1,2,0:T(1,128)}, u32[]{:S(2)}) %copy-start.2) | copy-done | bytes 72
  13.0 0.8 %pack_tokens.1 = (bf16[2,128,384]{2,1,0:T(8,128)(2,1)S(1)}, bf16[2,128,384]{2,1,0:T(8,128)(2,1)S(1)}, bf16[2,128,384]{2,1,0:T(8,128)(2,1)S(1)}, bf16[2,128,384]{2,1,0:T(8,128)(2,1)S(1)}, s32[12]{0:T(128)S(4)}) custom-call(s32[12]{0:T(128)S(1)} %bitcast.12, bf16[128,1536]{1,0:T(8,128)(2,1)S(1)} %collective-permute-done.arrived_ref, ...), custom_call_target="tpu_custom_call" | custom-call | flops 15000000512 | bytes 1048576 | tf_op jit(solution)/shard_map/pack_tokens/pallas_call | solution.py:85
  13.9 3.4 %collective-permute-start.2 = (bf16[2,128,384]{2,1,0:T(8,128)(2,1)S(1)}, bf16[2,128,384]{2,1,0:T(8,128)(2,1)S(1)}, u32[]{:S(2)}, u32[]{:S(2)}) collective-permute-start(bf16[2,128,384]{2,1,0:T(8,128)(2,1)S(1)} %get-tuple-element.14), channel_id=1, source_target_pairs={{0,1},{1,2},{2,3},{3,0},{4,5},{5,6},{6,7},{7,4},{8,9},{9,10},{10,1... | collective-permute-start | bytes 589832 | tf_op jit(solution)/shard_map/ppermute | solution.py:206
  17.3 4.6 %collective-permute-start.3 = (bf16[2,128,384]{2,1,0:T(8,128)(2,1)S(1)}, bf16[2,128,384]{2,1,0:T(8,128)(2,1)S(1)}, u32[]{:S(2)}, u32[]{:S(2)}) collective-permute-start(bf16[2,128,384]{2,1,0:T(8,128)(2,1)S(1)} %get-tuple-element.15), channel_id=1, source_target_pairs={{0,2},{1,3},{2,0},{3,1},{4,6},{5,7},{6,4},{7,5},{8,10},{9,11},{10,... | collective-permute-start | bytes 589832 | tf_op jit(solution)/shard_map/ppermute | solution.py:206
  21.9 3.3 %collective-permute-start.4 = (bf16[2,128,384]{2,1,0:T(8,128)(2,1)S(1)}, bf16[2,128,384]{2,1,0:T(8,128)(2,1)S(1)}, u32[]{:S(2)}, u32[]{:S(2)}) collective-permute-start(bf16[2,128,384]{2,1,0:T(8,128)(2,1)S(1)} %get-tuple-element.16), channel_id=1, source_target_pairs={{0,3},{1,0},{2,1},{3,2},{4,7},{5,4},{6,5},{7,6},{8,11},{9,8},{10,9... | collective-permute-start | bytes 589832 | tf_op jit(solution)/shard_map/ppermute | solution.py:206
  25.3 3.1 %all-to-all-done = bf16[16,128,128]{2,1,0:T(8,128)(2,1)S(1)} async-done(((bf16[16,128,128]{2,1,0:T(8,128)(2,1)}), bf16[16,128,128]{2,1,0:T(8,128)(2,1)S(1)}, u32[]{:S(2)}, u32[]{:S(2)}) %all-to-all-start) | async-done | bytes 524320 | tf_op jit(solution)/shard_map/all_to_all | solution.py:201
  28.4 0.7 %select.1 = bf16[12,64,128]{2,1,0:T(8,128)(2,1)} custom-call(s32[12]{0:T(128)S(4)} %get-tuple-element.17.slot_ref, bf16[32,64,128]{2,1,0:T(8,128)(2,1)S(1)} %bitcast.10), custom_call_target="tpu_custom_call" | custom-call | tf_op jit(solution)/shard_map/select/pallas_call | solution.py:103
  29.1 4.3 %all-to-all-start.1 = ((bf16[4,192,128]{2,1,0:T(8,128)(2,1)}), bf16[4,192,128]{2,1,0:T(8,128)(2,1)S(1)}, u32[]{:S(2)}, u32[]{:S(2)}) async-start(bf16[4,192,128]{2,1,0:T(8,128)(2,1)} %bitcast.7), calls=%async_computation.1 | async-start | bytes 393216 | tf_op jit(solution)/shard_map/all_to_all | solution.py:201
  33.4 0.0 collective-permute-done.2.refs_1_
  33.4 0.0 collective-permute-done.3.refs_2_
  33.4 0.0 collective-permute-done.4.refs_3_
  33.4 0.4 gram.1.sums_ref
  33.8 6.6 %all-to-all-done.1 = bf16[4,192,128]{2,1,0:T(8,128)(2,1)S(1)} async-done(((bf16[4,192,128]{2,1,0:T(8,128)(2,1)}), bf16[4,192,128]{2,1,0:T(8,128)(2,1)S(1)}, u32[]{:S(2)}, u32[]{:S(2)}) %all-to-all-start.1) | async-done | bytes 196640 | tf_op jit(solution)/shard_map/all_to_all | solution.py:201
  40.4 3.1 %precondition.1 = f32[3,128,128]{2,1,0:T(8,128)S(1)} custom-call(f32[3,256,256]{2,1,0:T(8,128)S(1)} %gram.1.sums_ref, bf16[4,3,2,32,128]{4,3,2,1,0:T(8,128)(2,1)S(1)} %bitcast.11), custom_call_target="tpu_custom_call" | custom-call | tf_op jit(solution)/shard_map/precondition/pallas_call | solution.py:190
  43.5 14.4 %all_gather.3 = f32[12,128,128]{2,1,0:T(8,128)S(1)} all-gather(f32[3,128,128]{2,1,0:T(8,128)S(1)} %precondition.1), channel_id=1, replica_groups=mesh['section'=16,'tensor'=8,'dp'=4] {'dp'}, dimensions={0}, use_global_device_ids=true | all-gather | bytes 983040 | tf_op jit(solution)/shard_map/all_gather | solution.py:229
  57.9 0.9 %copy.9 = f32[1,12,128,128]{3,2,1,0:T(8,128)} copy(f32[1,12,128,128]{3,2,1,0:T(8,128)S(1)} %bitcast.13) | data formatting | bytes 1572864
Async XLA Ops:
  0.0 12.4 %collective-permute-start = (bf16[128,1536]{1,0:T(8,128)(2,1)}, bf16[128,1536]{1,0:T(8,128)(2,1)S(1)}, u32[]{:S(2)}, u32[]{:S(2)}) collective-permute-start(bf16[128,1536]{1,0:T(8,128)(2,1)} %bitcast.16), channel_id=1, source_target_pairs={{0,32},{32,64},{64,96},{96,128},{128,160},{160,192},{192,224},{224... | collective-permute-start | bytes 1179656 | tf_op jit(solution)/shard_map/ppermute | solution.py:206
  0.0 2.0 %copy-start.3 = (bf16[1,128,1536]{2,1,0:T(8,128)(2,1)S(1)}, bf16[1,128,1536]{2,1,0:T(8,128)(2,1)}, u32[]{:S(2)}) copy-start(bf16[1,128,1536]{2,1,0:T(8,128)(2,1)} %param.9) | copy-start | bytes 1179652
  2.0 10.4 %collective-permute-start.1 = (bf16[128,1536]{1,0:T(8,128)(2,1)S(1)}, bf16[128,1536]{1,0:T(8,128)(2,1)S(1)}, u32[]{:S(2)}, u32[]{:S(2)}) collective-permute-start(bf16[128,1536]{1,0:T(8,128)(2,1)S(1)} %bitcast.17), channel_id=1, source_target_pairs={{0,480},{32,0},{64,32},{96,64},{128,96},{160,128},{192,160},{224,1... | collective-permute-start | bytes 1179656 | tf_op jit(solution)/shard_map/ppermute | solution.py:206
  5.0 7.5 %copy-start = (bf16[128,1536]{1,0:T(8,128)(2,1)S(1)}, bf16[128,1536]{1,0:T(8,128)(2,1)}, u32[]{:S(2)}) copy-start(bf16[128,1536]{1,0:T(8,128)(2,1)} %embedded_ref.1) | copy-start | bytes 1179652
  5.0 7.5 %copy-start.1 = (bf16[128,1536]{1,0:T(8,128)(2,1)S(1)}, bf16[128,1536]{1,0:T(8,128)(2,1)}, u32[]{:S(2)}) copy-start(bf16[128,1536]{1,0:T(8,128)(2,1)} %loss_ref.1) | copy-start | bytes 1179652
  5.0 23.4 %all-to-all-start = ((bf16[16,128,128]{2,1,0:T(8,128)(2,1)}), bf16[16,128,128]{2,1,0:T(8,128)(2,1)S(1)}, u32[]{:S(2)}, u32[]{:S(2)}) async-start(bf16[16,128,128]{2,1,0:T(8,128)(2,1)} %bitcast.5), calls=%async_computation | async-start | bytes 1048576 | tf_op jit(solution)/shard_map/all_to_all | solution.py:201
  12.4 0.7 %copy-start.2 = (s32[1,12,1]{1,2,0:T(1,128)S(1)}, s32[1,12,1]{1,2,0:T(1,128)}, u32[]{:S(2)}) copy-start(s32[1,12,1]{1,2,0:T(1,128)} %param.11) | copy-start | bytes 148
  13.9 19.5 %collective-permute-start.2 = (bf16[2,128,384]{2,1,0:T(8,128)(2,1)S(1)}, bf16[2,128,384]{2,1,0:T(8,128)(2,1)S(1)}, u32[]{:S(2)}, u32[]{:S(2)}) collective-permute-start(bf16[2,128,384]{2,1,0:T(8,128)(2,1)S(1)} %get-tuple-element.14), channel_id=1, source_target_pairs={{0,1},{1,2},{2,3},{3,0},{4,5},{5,6},{6,7},{7,4},{8,9},{9,10},{10,1... | collective-permute-start | bytes 589832 | tf_op jit(solution)/shard_map/ppermute | solution.py:206
  17.3 16.1 %collective-permute-start.3 = (bf16[2,128,384]{2,1,0:T(8,128)(2,1)S(1)}, bf16[2,128,384]{2,1,0:T(8,128)(2,1)S(1)}, u32[]{:S(2)}, u32[]{:S(2)}) collective-permute-start(bf16[2,128,384]{2,1,0:T(8,128)(2,1)S(1)} %get-tuple-element.15), channel_id=1, source_target_pairs={{0,2},{1,3},{2,0},{3,1},{4,6},{5,7},{6,4},{7,5},{8,10},{9,11},{10,... | collective-permute-start | bytes 589832 | tf_op jit(solution)/shard_map/ppermute | solution.py:206
  21.9 11.5 %collective-permute-start.4 = (bf16[2,128,384]{2,1,0:T(8,128)(2,1)S(1)}, bf16[2,128,384]{2,1,0:T(8,128)(2,1)S(1)}, u32[]{:S(2)}, u32[]{:S(2)}) collective-permute-start(bf16[2,128,384]{2,1,0:T(8,128)(2,1)S(1)} %get-tuple-element.16), channel_id=1, source_target_pairs={{0,3},{1,0},{2,1},{3,2},{4,7},{5,4},{6,5},{7,6},{8,11},{9,8},{10,9... | collective-permute-start | bytes 589832 | tf_op jit(solution)/shard_map/ppermute | solution.py:206
  29.1 11.3 %all-to-all-start.1 = ((bf16[4,192,128]{2,1,0:T(8,128)(2,1)}), bf16[4,192,128]{2,1,0:T(8,128)(2,1)S(1)}, u32[]{:S(2)}, u32[]{:S(2)}) async-start(bf16[4,192,128]{2,1,0:T(8,128)(2,1)} %bitcast.7), calls=%async_computation.1 | async-start | bytes 393216 | tf_op jit(solution)/shard_map/all_to_all | solution.py:201

commit v3 on v2

v3 whole, which is shorter than its diff:
```python
import functools

import jax
import jax.numpy as jnp
from jax import lax
from jax.experimental import pallas as pl
from jax.experimental.pallas import tpu as pltpu
from jax.sharding import PartitionSpec as P

BLK = 128
NS_ITERS = 5
DAMPING = 0.1
DP = 4
TILE = BLK // DP
CORNER = TILE // 2


SMALL = pltpu.CompilerParams(vmem_limit_bytes=4 * 1024 * 1024)
ANY = pl.BlockSpec(memory_space=pl.ANY)
VMEM = pl.BlockSpec(memory_space=pltpu.VMEM)
SMEM = pl.BlockSpec(memory_space=pltpu.SMEM)


def run(copies, sems):
    made = [pltpu.make_async_copy(source, target, sems.at[i]) for i, (source, target) in enumerate(copies)]
    for copy in made:
        copy.start()
    for copy in made:
        copy.wait()


def lane_tile(shape):
    return lax.broadcasted_iota(jnp.int32, shape, len(shape) - 1) // TILE


def turned(value, tiles):
    if isinstance(tiles, int):
        shift = tiles * TILE % BLK
        return pltpu.roll(value, shift, value.ndim - 1) if shift else value
    return pltpu.roll(value, lax.rem(tiles * TILE + 2 * BLK, BLK), value.ndim - 1)


def pack_state_kernel(a_ref, g_ref, out_ref, strip, corner, sems):
    part = lax.axis_index("dp")
    odd = lax.rem(part, 2)
    rows = pl.ds(pl.multiple_of(part * TILE, TILE), TILE)
    half = pl.ds(pl.multiple_of(odd * TILE + lax.div(part, 2) * CORNER, CORNER), CORNER)
    copies = []
    for which, ref in enumerate((a_ref, g_ref)):
        copies.append((ref.at[:, rows, :], strip.at[which]))
        copies.append((ref.at[:, half, :], corner.at[which]))
    run(copies, sems)

    sections = out_ref.shape[0]
    a, g = (strip[which].astype(jnp.float32).reshape(-1, BLK) for which in range(2))
    pairs = jnp.where(lane_tile(a.shape) < 2, turned(a, -part), turned(g, 2 - part))
    out_ref[:, :2 * TILE] = pairs.astype(out_ref.dtype).reshape(sections, 2 * TILE, BLK)

    a, g = (corner[which].astype(jnp.float32).reshape(sections, 2, CORNER, BLK) for which in range(2))
    tile = lane_tile((sections * CORNER, BLK))
    last = jnp.zeros(tile.shape, jnp.float32)
    for place, source in enumerate((a[:, 0], g[:, 0], a[:, 1], g[:, 1])):
        last = jnp.where(tile == place, turned(source.reshape(tile.shape), place - 2 - odd), last)
    out_ref[:, 2 * TILE:] = last.astype(out_ref.dtype).reshape(sections, CORNER, BLK)


def pack_state(state_a, state_g):
    slots = state_a.shape[0]
    state_a = pltpu.with_memory_space_constraint(state_a, pltpu.HBM)
    state_g = pltpu.with_memory_space_constraint(state_g, pltpu.HBM)
    return pl.pallas_call(
        pack_state_kernel,
        out_shape=pltpu.VMEM((slots // 2, 2 * TILE + CORNER, BLK), state_a.dtype),
        in_specs=[ANY, ANY],
        out_specs=VMEM,
        scratch_shapes=[
            pltpu.VMEM((2, slots, TILE, BLK), state_a.dtype),
            pltpu.VMEM((2, slots, CORNER, BLK), state_a.dtype),
            pltpu.SemaphoreType.DMA((4,)),
        ],
        compiler_params=pltpu.CompilerParams(vmem_limit_bytes=6 * 1024 * 1024),
        name="pack_state",
    )(state_a, state_g)


def pack_tokens_kernel(assign_ref, arrived_ref, embedded_ref, returned_ref, loss_ref, *refs):
    send_refs, (slot_ref, holder_ref, sems, holder_sem) = refs[:DP], refs[DP:]
    holders = pltpu.make_async_copy(assign_ref, holder_ref, holder_sem)
    holders.start()
    width = send_refs[0].shape[2]
    section, part = lax.axis_index("section"), lax.axis_index("dp")
    last_section = lax.axis_size("section") - 1

    for first in (True, False):
        for last in (True, False):
            if first and last:
                continue

            @pl.when(((section == 0) == first) & ((section == last_section) == last))
            def _():
                copies = []
                for which, source in enumerate((embedded_ref if first else arrived_ref, loss_ref if last else returned_ref)):
                    for turn in range(DP):
                        start = pl.multiple_of(lax.rem(part + turn, DP) * width, width)
                        copies.append((source.at[:, pl.ds(start, width)], send_refs[turn].at[which]))
                run(copies, sems)

    holders.wait()
    for j in range(holder_ref.shape[0]):
        rank = jnp.int32(0)
        for earlier in range(j):
            rank = rank + (holder_ref[earlier] == holder_ref[j]).astype(jnp.int32)
        slot_ref[j] = holder_ref[j] * 2 + rank


def pack_tokens(assign, arrived, embedded, returned, loss_grad):
    tokens, features = arrived.shape
    shape = jax.ShapeDtypeStruct((2, tokens, features // DP), arrived.dtype)
    assign = pltpu.with_memory_space_constraint(assign, pltpu.HBM)
    return pl.pallas_call(
        pack_tokens_kernel,
        out_shape=(shape,) * DP + (pltpu.SMEM(assign.shape, jnp.int32),),
        in_specs=[ANY] * 5,
        out_specs=(ANY,) * DP + (SMEM,),
        scratch_shapes=[
            pltpu.SMEM(assign.shape, jnp.int32),
            pltpu.SemaphoreType.DMA((2 * DP,)),
            pltpu.SemaphoreType.DMA,
        ],
        compiler_params=SMALL,
        cost_estimate=pl.CostEstimate(flops=15 * 10**9, bytes_accessed=2**20, transcendentals=0),
        name="pack_tokens",
    )(assign, arrived, embedded, returned, loss_grad)


def select_kernel(slot_ref, got_ref, out_ref):
    blocks = slot_ref.shape[0] // DP
    low = lane_tile((CORNER, BLK)) < 2
    for part in range(DP):
        corners = []
        for j in range(blocks):
            slot = slot_ref[part * blocks + j]
            holder, rank = lax.div(slot, 2), lax.rem(slot, 2)
            mine = pl.ds(pl.multiple_of(rank * TILE, TILE), TILE)
            out_ref[part, j * TILE:(j + 1) * TILE] = got_ref[holder, mine, :]
            corner = got_ref[holder, 2 * TILE:, :].astype(jnp.float32)
            corners.append(turned(corner, 2 * lax.rem(rank + j, 2)))
        for j in range(0, blocks, 2):
            both = jnp.where(low, corners[j], corners[min(j + 1, blocks - 1)])
            start = blocks * TILE + j // 2 * CORNER
            out_ref[part, start:start + CORNER] = both.astype(out_ref.dtype)


def select(slot, got):
    blocks = slot.shape[0] // DP
    return pl.pallas_call(
        select_kernel,
        out_shape=jax.ShapeDtypeStruct((DP, blocks * TILE + (blocks + 1) // 2 * CORNER, BLK), got.dtype),
        in_specs=[SMEM, VMEM],
        out_specs=VMEM,
        compiler_params=SMALL,
        name="select",
    )(slot, got)


def symmetric(held_ref, blocks, j, which):
    tile = lane_tile((TILE, BLK))
    start = blocks * TILE + j // 2 * CORNER
    corners = [held_ref[part, start:start + CORNER].astype(jnp.float32) for part in range(DP)]
    rows = []
    for part in range(DP):
        strip = turned(held_ref[part, j * TILE:(j + 1) * TILE].astype(jnp.float32), part - 2 * which)
        row = jnp.where(tile == part, 0.5 * strip, jnp.where(tile == (part + 1) % DP, strip, 0.0))
        if part < 2:
            corner = jnp.concatenate([corners[part], corners[part + 2]], axis=0)
            row = jnp.where(tile == part + 2, turned(corner, 2 + part - 2 * (j % 2) - which), row)
        rows.append(row)
    upper = jnp.concatenate(rows, axis=0)
    return upper + upper.T


def halves(value):
    high = value.astype(jnp.bfloat16)
    low = (value - high.astype(jnp.float32)).astype(jnp.bfloat16)
    return high, low


def product(left, right):
    lhs = jnp.concatenate([left[0], left[0], left[1]], axis=1)
    rhs = jnp.concatenate([right[0], right[1], right[0]], axis=0)
    return jnp.dot(lhs, rhs, preferred_element_type=jnp.float32)


def gram_kernel(*refs):
    chunk_refs, out_ref = refs[:-1], refs[-1]
    for j in range(out_ref.shape[0]):
        columns = slice(j * BLK, (j + 1) * BLK)
        inputs = jnp.concatenate([ref[0, :, columns] for ref in chunk_refs], axis=0)
        grads = jnp.concatenate([ref[1, :, columns] for ref in chunk_refs], axis=0)
        both = jnp.concatenate([inputs, grads], axis=1)
        out_ref[j] = lax.dot_general(both, both, (((0,), (0,)), ((), ())), preferred_element_type=jnp.float32)


def gram(chunks):
    return pl.pallas_call(
        gram_kernel,
        out_shape=jax.ShapeDtypeStruct((chunks[0].shape[2] // BLK, 2 * BLK, 2 * BLK), jnp.float32),
        in_specs=[VMEM] * DP,
        out_specs=VMEM,
        compiler_params=pltpu.CompilerParams(vmem_limit_bytes=8 * 1024 * 1024),
        cost_estimate=pl.CostEstimate(flops=10**9, bytes_accessed=2**20, transcendentals=0),
        name="gram",
    )(*chunks)


def precondition_kernel(tokens_total, sums_ref, held_ref, out_ref):
    count = out_ref.shape[0]
    row = lax.broadcasted_iota(jnp.int32, (BLK, BLK), 0)
    column = lax.broadcasted_iota(jnp.int32, (BLK, BLK), 1)
    identity = (row == column).astype(jnp.float32)
    blocks = [(j, which) for j in range(count) for which in range(2)]
    bound, rest, inverse = {}, {}, {}
    for j, which in blocks:
        held = symmetric(held_ref, count, j, which)
        batch = sums_ref[j, BLK:, BLK:] if which else sums_ref[j, :BLK, :BLK] / tokens_total
        matrix = 0.5 * held + 0.5 * batch + DAMPING * identity
        bound[j, which] = jnp.max(jnp.sum(jnp.abs(matrix), axis=0, keepdims=True), axis=1, keepdims=True)
        rest[j, which] = identity - matrix / bound[j, which]
    for block in blocks:
        inverse[block] = identity + rest[block]
        parts = halves(rest[block])
        rest[block] = product(parts, parts)
    for step in range(1, NS_ITERS):
        for block in blocks:
            left, right = halves(rest[block]), halves(inverse[block])
            if step < NS_ITERS - 1:
                both = product(left, [jnp.concatenate([l, r], axis=1) for l, r in zip(left, right)])
                rest[block] = both[:, :BLK]
                inverse[block] = inverse[block] + both[:, BLK:]
            else:
                inverse[block] = inverse[block] + product(left, right)
    half_done = [
        product(halves(inverse[j, 0]), halves(sums_ref[j, :BLK, BLK:] / bound[j, 0])) for j in range(count)
    ]
    for j in range(count):
        out_ref[j] = product(halves(half_done[j]), halves(inverse[j, 1])) / bound[j, 1]


def precondition(sums, held, tokens_total):
    return pl.pallas_call(
        functools.partial(precondition_kernel, tokens_total),
        out_shape=jax.ShapeDtypeStruct((sums.shape[0], BLK, BLK), jnp.float32),
        in_specs=[VMEM, VMEM],
        out_specs=VMEM,
        compiler_params=pltpu.CompilerParams(vmem_limit_bytes=8 * 1024 * 1024),
        name="precondition",
    )(sums, held)


def spread(array, axis):
    return lax.all_to_all(array, axis, split_axis=0, concat_axis=0, tiled=True)


def hop(array, axis, by):
    size = lax.axis_size(axis)
    return lax.ppermute(array, axis, [(i, (i + by) % size) for i in range(size)])


def body(section_out, embedded, section_grad, loss_grad, assign, state_a, state_g):
    tokens = embedded.shape[0]
    arrived = hop(section_out[0], "section", 1)
    packed, section_grad = lax.optimization_barrier((pack_state(state_a[0], state_g[0]), section_grad))
    returned = hop(section_grad[0], "section", -1)
    got = spread(packed, "section")

    *sends, slot = pack_tokens(assign[0, :, 0], arrived, embedded, returned, loss_grad)
    chunks = [sends[0]] + [hop(sends[turn], "dp", turn) for turn in range(1, DP)]

    held = spread(select(slot, got), "dp")

    result = precondition(gram(chunks), held, tokens * DP)
    return lax.all_gather(result, "dp", axis=0, tiled=True)[None]


def solution(mesh):
    in_specs = (
        P("section", "dp", "tensor"),
        P("dp", "tensor"),
        P("section", "dp", "tensor"),
        P("dp", "tensor"),
        P("section", "tensor", None),
        P("section", "tensor", None, None),
        P("section", "tensor", None, None),
    )
    out_specs = P("section", "tensor", None, None)
    return jax.shard_map(body, mesh=mesh, in_specs=in_specs, out_specs=out_specs, check_vma=False)
```

time: 59.2 us -> 52.4 us (0.89)
  starting transfers between devices: 26 us -> 23.1 us
  waiting for transfers between devices: 9.71 us -> 8.43 us
  blocking collectives: 14.4 us -> 13.4 us
  Pallas kernels: 7.03 us -> 6.1 us
  local copies, waits for them, and re-layouts: 1.5 us -> 0.9 us
    all_to_all x2, waiting for transfers between devices: 9.69 us -> 5.33 us  [spread(): return lax.all_to_all(array, axis, split_axis=0, concat_axis=0, tiled=True)]
    ppermute x5, waiting for transfers between devices: 0.01 us -> 3.09 us  [hop(): lax.ppermute(array, axis, [(i, (i + by) % size) for i in range(size)])]
    all_to_all x2, starting transfers between devices: 11.7 us -> 8.81 us  [spread(): return lax.all_to_all(array, axis, split_axis=0, concat_axis=0, tiled=True)]
    pallas_call x1, Pallas kernels: 3.11 us -> 1.77 us  [precondition(): pl.pallas_call(functools.partial(precondition_kernel, tokens_total), out_...]
    all_gather x1, blocking collectives: 14.4 us -> 13.4 us  [body(): return lax.all_gather(result, 'dp', axis=0, tiled=True)[None]]
    unnamed x9, local copies, waits for them, and re-layouts: 1.5 us -> 0.9 us
  transfers between devices with their start and end apart: 7 -> 7, of which waited for: 2 -> 3; matrix products, arithmetic and copies ran while one was open for 0% -> 0% of each run, Pallas kernels for 7% -> 4%
where the time goes in v3:
time: 52.4 us; the launch traced here: 52 us
  starting transfers between devices  23.1 us (44%)
  blocking collectives  13.4 us (26%)
  waiting for transfers between devices  8.43 us (16%)
  Pallas kernels  6.1 us (12%)
  local copies, waits for them, and re-layouts  0.9 us (2%)
    ppermute x5, starting transfers between devices, hop(): lax.ppermute(array, axis, [(i, (i + by) % size) for i in range(size)])  14.3 us
    all_gather x1, blocking collectives, body(): return lax.all_gather(result, 'dp', axis=0, tiled=True)[None]  13.4 us
    all_to_all x2, starting transfers between devices, spread(): return lax.all_to_all(array, axis, split_axis=0, concat_axis=0, tiled=True)  8.81 us
    all_to_all x2, waiting for transfers between devices, spread(): return lax.all_to_all(array, axis, split_axis=0, concat_axis=0, tiled=True)  5.33 us
    ppermute x5, waiting for transfers between devices, hop(): lax.ppermute(array, axis, [(i, (i + by) % size) for i in range(size)])  3.09 us
    pallas_call x1, Pallas kernels, pack_state(): pl.pallas_call(pack_state_kernel, out_shape=pltpu.VMEM((slots // 2, 2 * T...  2.28 us
    pallas_call x1, Pallas kernels, precondition(): pl.pallas_call(functools.partial(precondition_kernel, tokens_total), out_...  1.77 us
  transfers between devices with their start and end apart: 7, of which 3 were waited for; matrix products, arithmetic and copies ran while one was open for 0% of the time, Pallas kernels for 4%

profile of v3, /device:TPU:448, one launch (start us, length us, event | category | flops | bytes accessed | tf_op | source)
XLA Modules:
  0.0 52.0 jit_solution(12307341087402841966)
XLA Ops:
  0.0 0.0 copy-start.2
  0.0 0.0 copy-start.3
  0.0 0.0 copy-start.1
  0.0 2.3 %pack_state.1 = bf16[16,80,128]{2,1,0:T(8,128)(2,1)} custom-call(bf16[32,128,128]{2,1,0:T(8,128)(2,1)} %bitcast.7, bf16[32,128,128]{2,1,0:T(8,128)(2,1)} %bitcast.8), custom_call_target="tpu_custom_call" | custom-call | tf_op jit(solution)/shard_map/pack_state/pallas_call | solution.py:71
  2.3 0.0 copy-start
  2.3 0.0 copy-done.2
  2.3 2.9 %collective-permute-start.1 = (bf16[128,1536]{1,0:T(8,128)(2,1)S(1)}, bf16[128,1536]{1,0:T(8,128)(2,1)S(1)}, u32[]{:S(2)}, u32[]{:S(2)}) collective-permute-start(bf16[128,1536]{1,0:T(8,128)(2,1)S(1)} %bitcast.9), channel_id=1, source_target_pairs={{0,480},{32,0},{64,32},{96,64},{128,96},{160,128},{192,160},{224,1... | collective-permute-start | bytes 1179656 | tf_op jit(solution)/shard_map/ppermute | solution.py:266
  5.2 0.0 copy-done.3
  5.2 0.0 collective-permute-start
  5.2 5.5 %all-to-all-start = ((bf16[16,80,128]{2,1,0:T(8,128)(2,1)}), bf16[16,80,128]{2,1,0:T(8,128)(2,1)S(1)}, u32[]{:S(2)}, u32[]{:S(2)}) async-start(bf16[16,80,128]{2,1,0:T(8,128)(2,1)} %pack_state.1), calls=%async_computation | async-start | bytes 655360 | tf_op jit(solution)/shard_map/all_to_all | solution.py:261
  10.7 0.0 collective-permute-done.1.returned_ref
  10.7 2.9 %collective-permute-done.arrived_ref = bf16[128,1536]{1,0:T(8,128)(2,1)S(1)} collective-permute-done((bf16[128,1536]{1,0:T(8,128)(2,1)S(1)}, bf16[128,1536]{1,0:T(8,128)(2,1)S(1)}, u32[]{:S(2)}, u32[]{:S(2)}) %collective-permute-start) | collective-permute-done | bytes 393248 | tf_op jit(solution)/shard_map/ppermute | solution.py:266
  13.7 0.0 copy-done.1
  13.7 0.0 copy-done
  13.7 0.8 %pack_tokens.1 = (bf16[2,128,384]{2,1,0:T(8,128)(2,1)S(1)}, bf16[2,128,384]{2,1,0:T(8,128)(2,1)S(1)}, bf16[2,128,384]{2,1,0:T(8,128)(2,1)S(1)}, bf16[2,128,384]{2,1,0:T(8,128)(2,1)S(1)}, s32[12]{0:T(128)S(4)}) custom-call(s32[12]{0:T(128)} %bitcast.11, bf16[128,1536]{1,0:T(8,128)(2,1)S(1)} %collective-permute-done.arrived_ref, ...), custom_call_target="tpu_custom_call" | custom-call | flops 15000000512 | bytes 1048576 | tf_op jit(solution)/shard_map/pack_tokens/pallas_call | solution.py:120
  14.5 3.4 %collective-permute-start.2 = (bf16[2,128,384]{2,1,0:T(8,128)(2,1)S(1)}, bf16[2,128,384]{2,1,0:T(8,128)(2,1)S(1)}, u32[]{:S(2)}, u32[]{:S(2)}) collective-permute-start(bf16[2,128,384]{2,1,0:T(8,128)(2,1)S(1)} %get-tuple-element.14), channel_id=1, source_target_pairs={{0,1},{1,2},{2,3},{3,0},{4,5},{5,6},{6,7},{7,4},{8,9},{9,10},{10,1... | collective-permute-start | bytes 589832 | tf_op jit(solution)/shard_map/ppermute | solution.py:266
  17.9 4.6 %collective-permute-start.3 = (bf16[2,128,384]{2,1,0:T(8,128)(2,1)S(1)}, bf16[2,128,384]{2,1,0:T(8,128)(2,1)S(1)}, u32[]{:S(2)}, u32[]{:S(2)}) collective-permute-start(bf16[2,128,384]{2,1,0:T(8,128)(2,1)S(1)} %get-tuple-element.15), channel_id=1, source_target_pairs={{0,2},{1,3},{2,0},{3,1},{4,6},{5,7},{6,4},{7,5},{8,10},{9,11},{10,... | collective-permute-start | bytes 589832 | tf_op jit(solution)/shard_map/ppermute | solution.py:266
  22.5 3.3 %collective-permute-start.4 = (bf16[2,128,384]{2,1,0:T(8,128)(2,1)S(1)}, bf16[2,128,384]{2,1,0:T(8,128)(2,1)S(1)}, u32[]{:S(2)}, u32[]{:S(2)}) collective-permute-start(bf16[2,128,384]{2,1,0:T(8,128)(2,1)S(1)} %get-tuple-element.16), channel_id=1, source_target_pairs={{0,3},{1,0},{2,1},{3,2},{4,7},{5,4},{6,5},{7,6},{8,11},{9,8},{10,9... | collective-permute-start | bytes 589832 | tf_op jit(solution)/shard_map/ppermute | solution.py:266
  25.9 0.0 all-to-all-done.got_ref
  25.9 0.8 %select.1 = bf16[4,128,128]{2,1,0:T(8,128)(2,1)} custom-call(s32[12]{0:T(128)S(4)} %get-tuple-element.17.slot_ref, bf16[16,80,128]{2,1,0:T(8,128)(2,1)S(1)} %all-to-all-done.got_ref), custom_call_target="tpu_custom_call" | custom-call | tf_op jit(solution)/shard_map/select/pallas_call | solution.py:156
  26.7 3.3 %all-to-all-start.1 = ((bf16[4,128,128]{2,1,0:T(8,128)(2,1)}), bf16[4,128,128]{2,1,0:T(8,128)(2,1)S(1)}, u32[]{:S(2)}, u32[]{:S(2)}) async-start(bf16[4,128,128]{2,1,0:T(8,128)(2,1)} %select.1), calls=%async_computation.1 | async-start | bytes 262144 | tf_op jit(solution)/shard_map/all_to_all | solution.py:261
  30.1 0.0 collective-permute-done.2.refs_1_
  30.1 0.0 collective-permute-done.3.refs_2_
  30.1 0.2 collective-permute-done.4.refs_3_
  30.3 0.4 gram.1.sums_ref
  30.7 5.3 %all-to-all-done.1.held_ref = bf16[4,128,128]{2,1,0:T(8,128)(2,1)S(1)} async-done(((bf16[4,128,128]{2,1,0:T(8,128)(2,1)}), bf16[4,128,128]{2,1,0:T(8,128)(2,1)S(1)}, u32[]{:S(2)}, u32[]{:S(2)}) %all-to-all-start.1) | async-done | bytes 131104 | tf_op jit(solution)/shard_map/all_to_all | solution.py:261
  36.0 1.8 %precondition.1 = f32[3,128,128]{2,1,0:T(8,128)S(1)} custom-call(f32[3,256,256]{2,1,0:T(8,128)S(1)} %gram.1.sums_ref, bf16[4,128,128]{2,1,0:T(8,128)(2,1)S(1)} %all-to-all-done.1.held_ref), custom_call_target="tpu_custom_call" | custom-call | tf_op jit(solution)/shard_map/precondition/pallas_call | solution.py:250
  37.8 13.4 %all_gather.3 = f32[12,128,128]{2,1,0:T(8,128)S(1)} all-gather(f32[3,128,128]{2,1,0:T(8,128)S(1)} %precondition.1), channel_id=1, replica_groups=mesh['section'=16,'tensor'=8,'dp'=4] {'dp'}, dimensions={0}, use_global_device_ids=true | all-gather | bytes 983040 | tf_op jit(solution)/shard_map/all_gather | solution.py:282
  51.2 0.9 %copy.9 = f32[1,12,128,128]{3,2,1,0:T(8,128)} copy(f32[1,12,128,128]{3,2,1,0:T(8,128)S(1)} %bitcast.6) | data formatting | bytes 1572864
Async XLA Ops:
  0.0 2.3 %copy-start.2 = (bf16[1,128,1536]{2,1,0:T(8,128)(2,1)S(1)}, bf16[1,128,1536]{2,1,0:T(8,128)(2,1)}, u32[]{:S(2)}) copy-start(bf16[1,128,1536]{2,1,0:T(8,128)(2,1)} %param.9) | copy-start | bytes 1179652
  0.0 5.2 %copy-start.3 = (bf16[1,128,1536]{2,1,0:T(8,128)(2,1)S(1)}, bf16[1,128,1536]{2,1,0:T(8,128)(2,1)}, u32[]{:S(2)}) copy-start(bf16[1,128,1536]{2,1,0:T(8,128)(2,1)} %param.7) | copy-start | bytes 1179652
  0.0 13.7 %copy-start.1 = (bf16[128,1536]{1,0:T(8,128)(2,1)S(1)}, bf16[128,1536]{1,0:T(8,128)(2,1)}, u32[]{:S(2)}) copy-start(bf16[128,1536]{1,0:T(8,128)(2,1)} %loss_ref.1) | copy-start | bytes 1179652
  2.3 11.4 %copy-start = (bf16[128,1536]{1,0:T(8,128)(2,1)S(1)}, bf16[128,1536]{1,0:T(8,128)(2,1)}, u32[]{:S(2)}) copy-start(bf16[128,1536]{1,0:T(8,128)(2,1)} %embedded_ref.1) | copy-start | bytes 1179652
  2.3 8.4 %collective-permute-start.1 = (bf16[128,1536]{1,0:T(8,128)(2,1)S(1)}, bf16[128,1536]{1,0:T(8,128)(2,1)S(1)}, u32[]{:S(2)}, u32[]{:S(2)}) collective-permute-start(bf16[128,1536]{1,0:T(8,128)(2,1)S(1)} %bitcast.9), channel_id=1, source_target_pairs={{0,480},{32,0},{64,32},{96,64},{128,96},{160,128},{192,160},{224,1... | collective-permute-start | bytes 1179656 | tf_op jit(solution)/shard_map/ppermute | solution.py:266
  5.2 8.4 %collective-permute-start = (bf16[128,1536]{1,0:T(8,128)(2,1)S(1)}, bf16[128,1536]{1,0:T(8,128)(2,1)S(1)}, u32[]{:S(2)}, u32[]{:S(2)}) collective-permute-start(bf16[128,1536]{1,0:T(8,128)(2,1)S(1)} %bitcast.10), channel_id=1, source_target_pairs={{0,32},{32,64},{64,96},{96,128},{128,160},{160,192},{192,224},{224... | collective-permute-start | bytes 1179656 | tf_op jit(solution)/shard_map/ppermute | solution.py:266
  5.2 20.7 %all-to-all-start = ((bf16[16,80,128]{2,1,0:T(8,128)(2,1)}), bf16[16,80,128]{2,1,0:T(8,128)(2,1)S(1)}, u32[]{:S(2)}, u32[]{:S(2)}) async-start(bf16[16,80,128]{2,1,0:T(8,128)(2,1)} %pack_state.1), calls=%async_computation | async-start | bytes 655360 | tf_op jit(solution)/shard_map/all_to_all | solution.py:261
  14.5 15.6 %collective-permute-start.2 = (bf16[2,128,384]{2,1,0:T(8,128)(2,1)S(1)}, bf16[2,128,384]{2,1,0:T(8,128)(2,1)S(1)}, u32[]{:S(2)}, u32[]{:S(2)}) collective-permute-start(bf16[2,128,384]{2,1,0:T(8,128)(2,1)S(1)} %get-tuple-element.14), channel_id=1, source_target_pairs={{0,1},{1,2},{2,3},{3,0},{4,5},{5,6},{6,7},{7,4},{8,9},{9,10},{10,1... | collective-permute-start | bytes 589832 | tf_op jit(solution)/shard_map/ppermute | solution.py:266
  17.9 12.2 %collective-permute-start.3 = (bf16[2,128,384]{2,1,0:T(8,128)(2,1)S(1)}, bf16[2,128,384]{2,1,0:T(8,128)(2,1)S(1)}, u32[]{:S(2)}, u32[]{:S(2)}) collective-permute-start(bf16[2,128,384]{2,1,0:T(8,128)(2,1)S(1)} %get-tuple-element.15), channel_id=1, source_target_pairs={{0,2},{1,3},{2,0},{3,1},{4,6},{5,7},{6,4},{7,5},{8,10},{9,11},{10,... | collective-permute-start | bytes 589832 | tf_op jit(solution)/shard_map/ppermute | solution.py:266
  22.5 7.7 %collective-permute-start.4 = (bf16[2,128,384]{2,1,0:T(8,128)(2,1)S(1)}, bf16[2,128,384]{2,1,0:T(8,128)(2,1)S(1)}, u32[]{:S(2)}, u32[]{:S(2)}) collective-permute-start(bf16[2,128,384]{2,1,0:T(8,128)(2,1)S(1)} %get-tuple-element.16), channel_id=1, source_target_pairs={{0,3},{1,0},{2,1},{3,2},{4,7},{5,4},{6,5},{7,6},{8,11},{9,8},{10,9... | collective-permute-start | bytes 589832 | tf_op jit(solution)/shard_map/ppermute | solution.py:266
  26.7 9.3 %all-to-all-start.1 = ((bf16[4,128,128]{2,1,0:T(8,128)(2,1)}), bf16[4,128,128]{2,1,0:T(8,128)(2,1)S(1)}, u32[]{:S(2)}, u32[]{:S(2)}) async-start(bf16[4,128,128]{2,1,0:T(8,128)(2,1)} %select.1), calls=%async_computation.1 | async-start | bytes 262144 | tf_op jit(solution)/shard_map/all_to_all | solution.py:261

commit v4 on v3

--- a/solution.py
+++ b/solution.py
@@ -13,6 +13,8 @@
 DP = 4
 TILE = BLK // DP
 CORNER = TILE // 2
+OCTAVES = 240
+SCALE_ROWS = 16
 
 
 SMALL = pltpu.CompilerParams(vmem_limit_bytes=4 * 1024 * 1024)
@@ -213,8 +215,53 @@
     )(*chunks)
 
 
+def coded(value):
+    bound = jnp.max(jnp.abs(value), axis=0, keepdims=True)
+    bound = jnp.maximum(bound * (1 + 2.0**-7), 1e-35).astype(jnp.bfloat16)
+    place = jnp.abs(value) * (OCTAVES / bound.astype(jnp.float32))
+    octave = jnp.floor(place)
+    code = jnp.exp2(octave - OCTAVES // 2) * (1 + (place - octave))
+    code = jnp.where(value < 0, -code, code).astype(jnp.bfloat16)
+    return code, jnp.broadcast_to(bound, (SCALE_ROWS, BLK))
+
+
+def decoded(code, bound):
+    code = code.astype(jnp.float32)
+    size = jnp.abs(code)
+    octave = jnp.floor(jnp.log2(size))
+    place = octave + (OCTAVES // 2 - 1) + size * jnp.exp2(-octave)
+    value = place * (bound.astype(jnp.float32) / OCTAVES)
+    return jnp.where(code < 0, -value, value)
+
+
+def decode_kernel(got_ref, out_ref, values, sems):
+    blocks = got_ref.shape[1]
+    copies = []
+    for part in range(DP):
+        for j in range(blocks):
+            at = part * blocks + j
+            values[at] = decoded(got_ref[part, j, :BLK], got_ref[part, j, BLK:BLK + 1])
+            copies.append(pltpu.make_async_copy(values.at[at], out_ref.at[at], sems.at[at]))
+            copies[-1].start()
+    for copy in copies:
+        copy.wait()
+
+
+def decode(got):
+    blocks = DP * got.shape[1]
+    return pl.pallas_call(
+        decode_kernel,
+        out_shape=pltpu.HBM((blocks, BLK, BLK), jnp.float32),
+        in_specs=[VMEM],
+        out_specs=ANY,
+        scratch_shapes=[pltpu.VMEM((blocks, BLK, BLK), jnp.float32), pltpu.SemaphoreType.DMA((blocks,))],
+        compiler_params=SMALL,
+        name="decode",
+    )(got)
+
+
 def precondition_kernel(tokens_total, sums_ref, held_ref, out_ref):
-    count = out_ref.shape[0]
+    count = out_ref.shape[1]
     row = lax.broadcasted_iota(jnp.int32, (BLK, BLK), 0)
     column = lax.broadcasted_iota(jnp.int32, (BLK, BLK), 1)
     identity = (row == column).astype(jnp.float32)
@@ -243,13 +290,16 @@
         product(halves(inverse[j, 0]), halves(sums_ref[j, :BLK, BLK:] / bound[j, 0])) for j in range(count)
     ]
     for j in range(count):
-        out_ref[j] = product(halves(half_done[j]), halves(inverse[j, 1])) / bound[j, 1]
+        code, scale = coded(product(halves(half_done[j]), halves(inverse[j, 1])) / bound[j, 1])
+        for part in range(DP):
+            out_ref[part, j, :BLK] = code
+            out_ref[part, j, BLK:] = scale
 
 
 def precondition(sums, held, tokens_total):
     return pl.pallas_call(
         functools.partial(precondition_kernel, tokens_total),
-        out_shape=jax.ShapeDtypeStruct((sums.shape[0], BLK, BLK), jnp.float32),
+        out_shape=jax.ShapeDtypeStruct((DP, sums.shape[0], BLK + SCALE_ROWS, BLK), jnp.bfloat16),
         in_specs=[VMEM, VMEM],
         out_specs=VMEM,
         compiler_params=pltpu.CompilerParams(vmem_limit_bytes=8 * 1024 * 1024),
@@ -279,7 +329,7 @@
     held = spread(select(slot, got), "dp")
 
     result = precondition(gram(chunks), held, tokens * DP)
-    return lax.all_gather(result, "dp", axis=0, tiled=True)[None]
+    return decode(spread(result, "dp"))[None]
 
 
 def solution(mesh):

time: 52.4 us -> 49.4 us (0.943)
  blocking collectives: 13.4 us -> 10 us
  Pallas kernels: 6.1 us -> 7.26 us
  local copies, waits for them, and re-layouts: 0.9 us -> 0.02 us
    all_gather x1 -> x0, blocking collectives: 13.4 us -> none  [body(): return lax.all_gather(result, 'dp', axis=0, tiled=True)[None]]
    all_to_all x0 -> x1, blocking collectives: none -> 10 us  [spread(): return lax.all_to_all(array, axis, split_axis=0, concat_axis=0, tiled=True)]
    pallas_call x0 -> x1, Pallas kernels: none -> 1.09 us  [decode(): pl.pallas_call(decode_kernel, out_shape=pltpu.HBM((blocks, BLK, BLK), jnp...]
    unnamed x9 -> x8, local copies, waits for them, and re-layouts: 0.9 us -> 0.02 us
where the time goes in v4:
time: 49.4 us; the launch traced here: 49 us
  starting transfers between devices  23.1 us (47%)
  blocking collectives  10 us (20%)
  waiting for transfers between devices  8.43 us (17%)
  Pallas kernels  7.26 us (15%)
    ppermute x5, starting transfers between devices, hop(): lax.ppermute(array, axis, [(i, (i + by) % size) for i in range(size)])  14.3 us
    all_to_all x1, blocking collectives, spread(): return lax.all_to_all(array, axis, split_axis=0, concat_axis=0, tiled=True)  10 us
    all_to_all x2, starting transfers between devices, spread(): return lax.all_to_all(array, axis, split_axis=0, concat_axis=0, tiled=True)  8.81 us
    all_to_all x2, waiting for transfers between devices, spread(): return lax.all_to_all(array, axis, split_axis=0, concat_axis=0, tiled=True)  5.33 us
    ppermute x5, waiting for transfers between devices, hop(): lax.ppermute(array, axis, [(i, (i + by) % size) for i in range(size)])  3.09 us
    pallas_call x1, Pallas kernels, pack_state(): pl.pallas_call(pack_state_kernel, out_shape=pltpu.VMEM((slots // 2, 2 * T...  2.28 us
    pallas_call x1, Pallas kernels, precondition(): pl.pallas_call(functools.partial(precondition_kernel, tokens_total), out_...  1.85 us
    pallas_call x1, Pallas kernels, decode(): pl.pallas_call(decode_kernel, out_shape=pltpu.HBM((blocks, BLK, BLK), jnp...  1.09 us
  transfers between devices with their start and end apart: 7, of which 3 were waited for; matrix products, arithmetic and copies ran while one was open for 0% of the time, Pallas kernels for 4%

profile of v4, /device:TPU:448, one launch (start us, length us, event | category | flops | bytes accessed | tf_op | source)
XLA Modules:
  0.0 49.0 jit_solution(17742237987769279206)
XLA Ops:
  0.0 0.0 copy-start.2
  0.0 0.0 copy-start.3
  0.0 0.0 copy-start.1
  0.0 2.3 %pack_state.1 = bf16[16,80,128]{2,1,0:T(8,128)(2,1)} custom-call(bf16[32,128,128]{2,1,0:T(8,128)(2,1)} %bitcast.6, bf16[32,128,128]{2,1,0:T(8,128)(2,1)} %bitcast.7), custom_call_target="tpu_custom_call" | custom-call | tf_op jit(solution)/shard_map/pack_state/pallas_call | solution.py:73
  2.3 0.0 copy-start
  2.3 0.0 copy-done.2
  2.3 2.9 %collective-permute-start.1 = (bf16[128,1536]{1,0:T(8,128)(2,1)S(1)}, bf16[128,1536]{1,0:T(8,128)(2,1)S(1)}, u32[]{:S(2)}, u32[]{:S(2)}) collective-permute-start(bf16[128,1536]{1,0:T(8,128)(2,1)S(1)} %bitcast.8), channel_id=1, source_target_pairs={{0,480},{32,0},{64,32},{96,64},{128,96},{160,128},{192,160},{224,1... | collective-permute-start | bytes 1179656 | tf_op jit(solution)/shard_map/ppermute | solution.py:316
  5.2 0.0 copy-done.3
  5.2 0.0 collective-permute-start
  5.2 5.5 %all-to-all-start = ((bf16[16,80,128]{2,1,0:T(8,128)(2,1)}), bf16[16,80,128]{2,1,0:T(8,128)(2,1)S(1)}, u32[]{:S(2)}, u32[]{:S(2)}) async-start(bf16[16,80,128]{2,1,0:T(8,128)(2,1)} %pack_state.1), calls=%async_computation | async-start | bytes 655360 | tf_op jit(solution)/shard_map/all_to_all | solution.py:311
  10.7 0.0 collective-permute-done.1.returned_ref
  10.7 2.9 %collective-permute-done.arrived_ref = bf16[128,1536]{1,0:T(8,128)(2,1)S(1)} collective-permute-done((bf16[128,1536]{1,0:T(8,128)(2,1)S(1)}, bf16[128,1536]{1,0:T(8,128)(2,1)S(1)}, u32[]{:S(2)}, u32[]{:S(2)}) %collective-permute-start) | collective-permute-done | bytes 393248 | tf_op jit(solution)/shard_map/ppermute | solution.py:316
  13.7 0.0 copy-done.1
  13.7 0.0 copy-done
  13.7 0.8 %pack_tokens.1 = (bf16[2,128,384]{2,1,0:T(8,128)(2,1)S(1)}, bf16[2,128,384]{2,1,0:T(8,128)(2,1)S(1)}, bf16[2,128,384]{2,1,0:T(8,128)(2,1)S(1)}, bf16[2,128,384]{2,1,0:T(8,128)(2,1)S(1)}, s32[12]{0:T(128)S(4)}) custom-call(s32[12]{0:T(128)} %bitcast.10, bf16[128,1536]{1,0:T(8,128)(2,1)S(1)} %collective-permute-done.arrived_ref, ...), custom_call_target="tpu_custom_call" | custom-call | flops 15000000512 | bytes 1048576 | tf_op jit(solution)/shard_map/pack_tokens/pallas_call | solution.py:122
  14.5 3.4 %collective-permute-start.2 = (bf16[2,128,384]{2,1,0:T(8,128)(2,1)S(1)}, bf16[2,128,384]{2,1,0:T(8,128)(2,1)S(1)}, u32[]{:S(2)}, u32[]{:S(2)}) collective-permute-start(bf16[2,128,384]{2,1,0:T(8,128)(2,1)S(1)} %get-tuple-element.14), channel_id=1, source_target_pairs={{0,1},{1,2},{2,3},{3,0},{4,5},{5,6},{6,7},{7,4},{8,9},{9,10},{10,1... | collective-permute-start | bytes 589832 | tf_op jit(solution)/shard_map/ppermute | solution.py:316
  17.9 4.6 %collective-permute-start.3 = (bf16[2,128,384]{2,1,0:T(8,128)(2,1)S(1)}, bf16[2,128,384]{2,1,0:T(8,128)(2,1)S(1)}, u32[]{:S(2)}, u32[]{:S(2)}) collective-permute-start(bf16[2,128,384]{2,1,0:T(8,128)(2,1)S(1)} %get-tuple-element.15), channel_id=1, source_target_pairs={{0,2},{1,3},{2,0},{3,1},{4,6},{5,7},{6,4},{7,5},{8,10},{9,11},{10,... | collective-permute-start | bytes 589832 | tf_op jit(solution)/shard_map/ppermute | solution.py:316
  22.5 3.3 %collective-permute-start.4 = (bf16[2,128,384]{2,1,0:T(8,128)(2,1)S(1)}, bf16[2,128,384]{2,1,0:T(8,128)(2,1)S(1)}, u32[]{:S(2)}, u32[]{:S(2)}) collective-permute-start(bf16[2,128,384]{2,1,0:T(8,128)(2,1)S(1)} %get-tuple-element.16), channel_id=1, source_target_pairs={{0,3},{1,0},{2,1},{3,2},{4,7},{5,4},{6,5},{7,6},{8,11},{9,8},{10,9... | collective-permute-start | bytes 589832 | tf_op jit(solution)/shard_map/ppermute | solution.py:316
  25.9 0.0 all-to-all-done.got_ref
  25.9 0.8 %select.1 = bf16[4,128,128]{2,1,0:T(8,128)(2,1)} custom-call(s32[12]{0:T(128)S(4)} %get-tuple-element.17.slot_ref, bf16[16,80,128]{2,1,0:T(8,128)(2,1)S(1)} %all-to-all-done.got_ref), custom_call_target="tpu_custom_call" | custom-call | tf_op jit(solution)/shard_map/select/pallas_call | solution.py:158
  26.7 3.3 %all-to-all-start.1 = ((bf16[4,128,128]{2,1,0:T(8,128)(2,1)}), bf16[4,128,128]{2,1,0:T(8,128)(2,1)S(1)}, u32[]{:S(2)}, u32[]{:S(2)}) async-start(bf16[4,128,128]{2,1,0:T(8,128)(2,1)} %select.1), calls=%async_computation.1 | async-start | bytes 262144 | tf_op jit(solution)/shard_map/all_to_all | solution.py:311
  30.1 0.0 collective-permute-done.2.refs_1_
  30.1 0.0 collective-permute-done.3.refs_2_
  30.1 0.2 collective-permute-done.4.refs_3_
  30.3 0.4 gram.1.sums_ref
  30.7 5.3 %all-to-all-done.1.held_ref = bf16[4,128,128]{2,1,0:T(8,128)(2,1)S(1)} async-done(((bf16[4,128,128]{2,1,0:T(8,128)(2,1)}), bf16[4,128,128]{2,1,0:T(8,128)(2,1)S(1)}, u32[]{:S(2)}, u32[]{:S(2)}) %all-to-all-start.1) | async-done | bytes 131104 | tf_op jit(solution)/shard_map/all_to_all | solution.py:311
  36.0 1.8 %precondition.1 = bf16[4,3,144,128]{3,2,1,0:T(8,128)(2,1)S(1)} custom-call(f32[3,256,256]{2,1,0:T(8,128)S(1)} %gram.1.sums_ref, bf16[4,128,128]{2,1,0:T(8,128)(2,1)S(1)} %all-to-all-done.1.held_ref), custom_call_target="tpu_custom_call" | custom-call | tf_op jit(solution)/shard_map/precondition/pallas_call | solution.py:300
  37.9 10.0 %all_to_all.15.got_ref = bf16[4,3,144,128]{3,2,1,0:T(8,128)(2,1)S(1)} all-to-all(bf16[4,3,144,128]{3,2,1,0:T(8,128)(2,1)S(1)} %precondition.1), channel_id=1, replica_groups=mesh['section'=16,'tensor'=8,'dp'=4] {'dp'}, dimensions={0} | all-to-all | bytes 884736 | tf_op jit(solution)/shard_map/all_to_all | solution.py:311
  47.9 1.1 %decode.1 = f32[12,128,128]{2,1,0:T(8,128)} custom-call(bf16[4,3,144,128]{3,2,1,0:T(8,128)(2,1)S(1)} %all_to_all.15.got_ref), custom_call_target="tpu_custom_call" | custom-call | tf_op jit(solution)/shard_map/decode/pallas_call | solution.py:252
Async XLA Ops:
  0.0 2.3 %copy-start.2 = (bf16[1,128,1536]{2,1,0:T(8,128)(2,1)S(1)}, bf16[1,128,1536]{2,1,0:T(8,128)(2,1)}, u32[]{:S(2)}) copy-start(bf16[1,128,1536]{2,1,0:T(8,128)(2,1)} %param.9) | copy-start | bytes 1179652
  0.0 5.2 %copy-start.3 = (bf16[1,128,1536]{2,1,0:T(8,128)(2,1)S(1)}, bf16[1,128,1536]{2,1,0:T(8,128)(2,1)}, u32[]{:S(2)}) copy-start(bf16[1,128,1536]{2,1,0:T(8,128)(2,1)} %param.7) | copy-start | bytes 1179652
  0.0 13.7 %copy-start.1 = (bf16[128,1536]{1,0:T(8,128)(2,1)S(1)}, bf16[128,1536]{1,0:T(8,128)(2,1)}, u32[]{:S(2)}) copy-start(bf16[128,1536]{1,0:T(8,128)(2,1)} %loss_ref.1) | copy-start | bytes 1179652
  2.3 11.4 %copy-start = (bf16[128,1536]{1,0:T(8,128)(2,1)S(1)}, bf16[128,1536]{1,0:T(8,128)(2,1)}, u32[]{:S(2)}) copy-start(bf16[128,1536]{1,0:T(8,128)(2,1)} %embedded_ref.1) | copy-start | bytes 1179652
  2.3 8.4 %collective-permute-start.1 = (bf16[128,1536]{1,0:T(8,128)(2,1)S(1)}, bf16[128,1536]{1,0:T(8,128)(2,1)S(1)}, u32[]{:S(2)}, u32[]{:S(2)}) collective-permute-start(bf16[128,1536]{1,0:T(8,128)(2,1)S(1)} %bitcast.8), channel_id=1, source_target_pairs={{0,480},{32,0},{64,32},{96,64},{128,96},{160,128},{192,160},{224,1... | collective-permute-start | bytes 1179656 | tf_op jit(solution)/shard_map/ppermute | solution.py:316
  5.2 8.4 %collective-permute-start = (bf16[128,1536]{1,0:T(8,128)(2,1)S(1)}, bf16[128,1536]{1,0:T(8,128)(2,1)S(1)}, u32[]{:S(2)}, u32[]{:S(2)}) collective-permute-start(bf16[128,1536]{1,0:T(8,128)(2,1)S(1)} %bitcast.9), channel_id=1, source_target_pairs={{0,32},{32,64},{64,96},{96,128},{128,160},{160,192},{192,224},{224... | collective-permute-start | bytes 1179656 | tf_op jit(solution)/shard_map/ppermute | solution.py:316
  5.2 20.7 %all-to-all-start = ((bf16[16,80,128]{2,1,0:T(8,128)(2,1)}), bf16[16,80,128]{2,1,0:T(8,128)(2,1)S(1)}, u32[]{:S(2)}, u32[]{:S(2)}) async-start(bf16[16,80,128]{2,1,0:T(8,128)(2,1)} %pack_state.1), calls=%async_computation | async-start | bytes 655360 | tf_op jit(solution)/shard_map/all_to_all | solution.py:311
  14.5 15.6 %collective-permute-start.2 = (bf16[2,128,384]{2,1,0:T(8,128)(2,1)S(1)}, bf16[2,128,384]{2,1,0:T(8,128)(2,1)S(1)}, u32[]{:S(2)}, u32[]{:S(2)}) collective-permute-start(bf16[2,128,384]{2,1,0:T(8,128)(2,1)S(1)} %get-tuple-element.14), channel_id=1, source_target_pairs={{0,1},{1,2},{2,3},{3,0},{4,5},{5,6},{6,7},{7,4},{8,9},{9,10},{10,1... | collective-permute-start | bytes 589832 | tf_op jit(solution)/shard_map/ppermute | solution.py:316
  17.9 12.2 %collective-permute-start.3 = (bf16[2,128,384]{2,1,0:T(8,128)(2,1)S(1)}, bf16[2,128,384]{2,1,0:T(8,128)(2,1)S(1)}, u32[]{:S(2)}, u32[]{:S(2)}) collective-permute-start(bf16[2,128,384]{2,1,0:T(8,128)(2,1)S(1)} %get-tuple-element.15), channel_id=1, source_target_pairs={{0,2},{1,3},{2,0},{3,1},{4,6},{5,7},{6,4},{7,5},{8,10},{9,11},{10,... | collective-permute-start | bytes 589832 | tf_op jit(solution)/shard_map/ppermute | solution.py:316
  22.5 7.7 %collective-permute-start.4 = (bf16[2,128,384]{2,1,0:T(8,128)(2,1)S(1)}, bf16[2,128,384]{2,1,0:T(8,128)(2,1)S(1)}, u32[]{:S(2)}, u32[]{:S(2)}) collective-permute-start(bf16[2,128,384]{2,1,0:T(8,128)(2,1)S(1)} %get-tuple-element.16), channel_id=1, source_target_pairs={{0,3},{1,0},{2,1},{3,2},{4,7},{5,4},{6,5},{7,6},{8,11},{9,8},{10,9... | collective-permute-start | bytes 589832 | tf_op jit(solution)/shard_map/ppermute | solution.py:316
  26.7 9.3 %all-to-all-start.1 = ((bf16[4,128,128]{2,1,0:T(8,128)(2,1)}), bf16[4,128,128]{2,1,0:T(8,128)(2,1)S(1)}, u32[]{:S(2)}, u32[]{:S(2)}) async-start(bf16[4,128,128]{2,1,0:T(8,128)(2,1)} %select.1), calls=%async_computation.1 | async-start | bytes 262144 | tf_op jit(solution)/shard_map/all_to_all | solution.py:311

commit v5 on v4

--- a/solution.py
+++ b/solution.py
@@ -146,7 +146,7 @@
             mine = pl.ds(pl.multiple_of(rank * TILE, TILE), TILE)
             out_ref[part, j * TILE:(j + 1) * TILE] = got_ref[holder, mine, :]
             corner = got_ref[holder, 2 * TILE:, :].astype(jnp.float32)
-            corners.append(turned(corner, 2 * lax.rem(rank + j, 2)))
+            corners.append(jnp.where(lax.rem(rank + j, 2) == 1, turned(corner, 2), corner))
         for j in range(0, blocks, 2):
             both = jnp.where(low, corners[j], corners[min(j + 1, blocks - 1)])
             start = blocks * TILE + j // 2 * CORNER
@@ -222,7 +222,7 @@
     octave = jnp.floor(place)
     code = jnp.exp2(octave - OCTAVES // 2) * (1 + (place - octave))
     code = jnp.where(value < 0, -code, code).astype(jnp.bfloat16)
-    return code, jnp.broadcast_to(bound, (SCALE_ROWS, BLK))
+    return code, bound
 
 
 def decoded(code, bound):
@@ -230,17 +230,18 @@
     size = jnp.abs(code)
     octave = jnp.floor(jnp.log2(size))
     place = octave + (OCTAVES // 2 - 1) + size * jnp.exp2(-octave)
-    value = place * (bound.astype(jnp.float32) / OCTAVES)
+    value = place * (bound / OCTAVES)
     return jnp.where(code < 0, -value, value)
 
 
 def decode_kernel(got_ref, out_ref, values, sems):
-    blocks = got_ref.shape[1]
+    blocks = got_ref.shape[1] // BLK
     copies = []
     for part in range(DP):
+        scales = got_ref[part, blocks * BLK:].astype(jnp.float32)
         for j in range(blocks):
             at = part * blocks + j
-            values[at] = decoded(got_ref[part, j, :BLK], got_ref[part, j, BLK:BLK + 1])
+            values[at] = decoded(got_ref[part, j * BLK:(j + 1) * BLK], scales[j:j + 1])
             copies.append(pltpu.make_async_copy(values.at[at], out_ref.at[at], sems.at[at]))
             copies[-1].start()
     for copy in copies:
@@ -248,7 +249,7 @@
 
 
 def decode(got):
-    blocks = DP * got.shape[1]
+    blocks = DP * (got.shape[1] // BLK)
     return pl.pallas_call(
         decode_kernel,
         out_shape=pltpu.HBM((blocks, BLK, BLK), jnp.float32),
@@ -261,18 +262,19 @@
 
 
 def precondition_kernel(tokens_total, sums_ref, held_ref, out_ref):
-    count = out_ref.shape[1]
+    count = out_ref.shape[1] // BLK
     row = lax.broadcasted_iota(jnp.int32, (BLK, BLK), 0)
     column = lax.broadcasted_iota(jnp.int32, (BLK, BLK), 1)
     identity = (row == column).astype(jnp.float32)
     blocks = [(j, which) for j in range(count) for which in range(2)]
-    bound, rest, inverse = {}, {}, {}
+    scale, rest, inverse = {}, {}, {}
     for j, which in blocks:
         held = symmetric(held_ref, count, j, which)
-        batch = sums_ref[j, BLK:, BLK:] if which else sums_ref[j, :BLK, :BLK] / tokens_total
+        batch = sums_ref[j, BLK:, BLK:] if which else sums_ref[j, :BLK, :BLK] * (1 / tokens_total)
         matrix = 0.5 * held + 0.5 * batch + DAMPING * identity
-        bound[j, which] = jnp.max(jnp.sum(jnp.abs(matrix), axis=0, keepdims=True), axis=1, keepdims=True)
-        rest[j, which] = identity - matrix / bound[j, which]
+        bound = jnp.max(jnp.sum(jnp.abs(matrix), axis=0, keepdims=True), axis=1, keepdims=True)
+        scale[j, which] = 1 / bound
+        rest[j, which] = identity - matrix * scale[j, which]
     for block in blocks:
         inverse[block] = identity + rest[block]
         parts = halves(rest[block])
@@ -287,19 +289,22 @@
             else:
                 inverse[block] = inverse[block] + product(left, right)
     half_done = [
-        product(halves(inverse[j, 0]), halves(sums_ref[j, :BLK, BLK:] / bound[j, 0])) for j in range(count)
+        product(halves(inverse[j, 0]), halves(sums_ref[j, :BLK, BLK:] * scale[j, 0])) for j in range(count)
     ]
+    tops = jnp.zeros((SCALE_ROWS, BLK), jnp.float32)
     for j in range(count):
-        code, scale = coded(product(halves(half_done[j]), halves(inverse[j, 1])) / bound[j, 1])
+        code, top = coded(product(halves(half_done[j]), halves(inverse[j, 1])) * scale[j, 1])
+        tops = jnp.where(row[:SCALE_ROWS] == j, top.astype(jnp.float32), tops)
         for part in range(DP):
-            out_ref[part, j, :BLK] = code
-            out_ref[part, j, BLK:] = scale
+            out_ref[part, j * BLK:(j + 1) * BLK] = code
+    for part in range(DP):
+        out_ref[part, count * BLK:] = tops.astype(out_ref.dtype)
 
 
 def precondition(sums, held, tokens_total):
     return pl.pallas_call(
         functools.partial(precondition_kernel, tokens_total),
-        out_shape=jax.ShapeDtypeStruct((DP, sums.shape[0], BLK + SCALE_ROWS, BLK), jnp.bfloat16),
+        out_shape=jax.ShapeDtypeStruct((DP, sums.shape[0] * BLK + SCALE_ROWS, BLK), jnp.bfloat16),
         in_specs=[VMEM, VMEM],
         out_specs=VMEM,
         compiler_params=pltpu.CompilerParams(vmem_limit_bytes=8 * 1024 * 1024),

time: 49.4 us -> 49.2 us (level)
  no operation moved by 1% of the time
where the time goes in v5:
time: 49.2 us; the launch traced here: 48.7 us
  starting transfers between devices  23.1 us (47%)
  blocking collectives  9.83 us (20%)
  waiting for transfers between devices  8.43 us (17%)
  Pallas kernels  7.23 us (15%)
    ppermute x5, starting transfers between devices, hop(): lax.ppermute(array, axis, [(i, (i + by) % size) for i in range(size)])  14.3 us
    all_to_all x1, blocking collectives, spread(): return lax.all_to_all(array, axis, split_axis=0, concat_axis=0, tiled=True)  9.83 us
    all_to_all x2, starting transfers between devices, spread(): return lax.all_to_all(array, axis, split_axis=0, concat_axis=0, tiled=True)  8.81 us
    all_to_all x2, waiting for transfers between devices, spread(): return lax.all_to_all(array, axis, split_axis=0, concat_axis=0, tiled=True)  5.31 us
    ppermute x5, waiting for transfers between devices, hop(): lax.ppermute(array, axis, [(i, (i + by) % size) for i in range(size)])  3.12 us
    pallas_call x1, Pallas kernels, pack_state(): pl.pallas_call(pack_state_kernel, out_shape=pltpu.VMEM((slots // 2, 2 * T...  2.28 us
    pallas_call x1, Pallas kernels, precondition(): pl.pallas_call(functools.partial(precondition_kernel, tokens_total), out_...  1.85 us
    pallas_call x1, Pallas kernels, decode(): pl.pallas_call(decode_kernel, out_shape=pltpu.HBM((blocks, BLK, BLK), jnp...  1.08 us
  transfers between devices with their start and end apart: 7, of which 3 were waited for; matrix products, arithmetic and copies ran while one was open for 0% of the time, Pallas kernels for 4%

profile of v5, /device:TPU:448, one launch (start us, length us, event | category | flops | bytes accessed | tf_op | source)
XLA Modules:
  0.0 48.7 jit_solution(1569382683202596151)
XLA Ops:
  0.0 0.0 copy-start.2
  0.0 0.0 copy-start.3
  0.0 0.0 copy-start.1
  0.0 2.3 %pack_state.1 = bf16[16,80,128]{2,1,0:T(8,128)(2,1)} custom-call(bf16[32,128,128]{2,1,0:T(8,128)(2,1)} %bitcast.6, bf16[32,128,128]{2,1,0:T(8,128)(2,1)} %bitcast.7), custom_call_target="tpu_custom_call" | custom-call | tf_op jit(solution)/shard_map/pack_state/pallas_call | solution.py:73
  2.3 0.0 copy-start
  2.3 0.0 copy-done.2
  2.3 2.9 %collective-permute-start.1 = (bf16[128,1536]{1,0:T(8,128)(2,1)S(1)}, bf16[128,1536]{1,0:T(8,128)(2,1)S(1)}, u32[]{:S(2)}, u32[]{:S(2)}) collective-permute-start(bf16[128,1536]{1,0:T(8,128)(2,1)S(1)} %bitcast.8), channel_id=1, source_target_pairs={{0,480},{32,0},{64,32},{96,64},{128,96},{160,128},{192,160},{224,1... | collective-permute-start | bytes 1179656 | tf_op jit(solution)/shard_map/ppermute | solution.py:321
  5.2 0.0 copy-done.3
  5.2 0.0 collective-permute-start
  5.2 5.5 %all-to-all-start = ((bf16[16,80,128]{2,1,0:T(8,128)(2,1)}), bf16[16,80,128]{2,1,0:T(8,128)(2,1)S(1)}, u32[]{:S(2)}, u32[]{:S(2)}) async-start(bf16[16,80,128]{2,1,0:T(8,128)(2,1)} %pack_state.1), calls=%async_computation | async-start | bytes 655360 | tf_op jit(solution)/shard_map/all_to_all | solution.py:316
  10.7 0.0 collective-permute-done.1.returned_ref
  10.7 2.9 %collective-permute-done.arrived_ref = bf16[128,1536]{1,0:T(8,128)(2,1)S(1)} collective-permute-done((bf16[128,1536]{1,0:T(8,128)(2,1)S(1)}, bf16[128,1536]{1,0:T(8,128)(2,1)S(1)}, u32[]{:S(2)}, u32[]{:S(2)}) %collective-permute-start) | collective-permute-done | bytes 393248 | tf_op jit(solution)/shard_map/ppermute | solution.py:321
  13.7 0.0 copy-done.1
  13.7 0.0 copy-done
  13.7 0.8 %pack_tokens.1 = (bf16[2,128,384]{2,1,0:T(8,128)(2,1)S(1)}, bf16[2,128,384]{2,1,0:T(8,128)(2,1)S(1)}, bf16[2,128,384]{2,1,0:T(8,128)(2,1)S(1)}, bf16[2,128,384]{2,1,0:T(8,128)(2,1)S(1)}, s32[12]{0:T(128)S(4)}) custom-call(s32[12]{0:T(128)} %bitcast.10, bf16[128,1536]{1,0:T(8,128)(2,1)S(1)} %collective-permute-done.arrived_ref, ...), custom_call_target="tpu_custom_call" | custom-call | flops 15000000512 | bytes 1048576 | tf_op jit(solution)/shard_map/pack_tokens/pallas_call | solution.py:122
  14.5 3.4 %collective-permute-start.2 = (bf16[2,128,384]{2,1,0:T(8,128)(2,1)S(1)}, bf16[2,128,384]{2,1,0:T(8,128)(2,1)S(1)}, u32[]{:S(2)}, u32[]{:S(2)}) collective-permute-start(bf16[2,128,384]{2,1,0:T(8,128)(2,1)S(1)} %get-tuple-element.14), channel_id=1, source_target_pairs={{0,1},{1,2},{2,3},{3,0},{4,5},{5,6},{6,7},{7,4},{8,9},{9,10},{10,1... | collective-permute-start | bytes 589832 | tf_op jit(solution)/shard_map/ppermute | solution.py:321
  17.9 4.6 %collective-permute-start.3 = (bf16[2,128,384]{2,1,0:T(8,128)(2,1)S(1)}, bf16[2,128,384]{2,1,0:T(8,128)(2,1)S(1)}, u32[]{:S(2)}, u32[]{:S(2)}) collective-permute-start(bf16[2,128,384]{2,1,0:T(8,128)(2,1)S(1)} %get-tuple-element.15), channel_id=1, source_target_pairs={{0,2},{1,3},{2,0},{3,1},{4,6},{5,7},{6,4},{7,5},{8,10},{9,11},{10,... | collective-permute-start | bytes 589832 | tf_op jit(solution)/shard_map/ppermute | solution.py:321
  22.5 3.3 %collective-permute-start.4 = (bf16[2,128,384]{2,1,0:T(8,128)(2,1)S(1)}, bf16[2,128,384]{2,1,0:T(8,128)(2,1)S(1)}, u32[]{:S(2)}, u32[]{:S(2)}) collective-permute-start(bf16[2,128,384]{2,1,0:T(8,128)(2,1)S(1)} %get-tuple-element.16), channel_id=1, source_target_pairs={{0,3},{1,0},{2,1},{3,2},{4,7},{5,4},{6,5},{7,6},{8,11},{9,8},{10,9... | collective-permute-start | bytes 589832 | tf_op jit(solution)/shard_map/ppermute | solution.py:321
  25.9 0.0 all-to-all-done.got_ref
  25.9 0.8 %select.1 = bf16[4,128,128]{2,1,0:T(8,128)(2,1)} custom-call(s32[12]{0:T(128)S(4)} %get-tuple-element.17.slot_ref, bf16[16,80,128]{2,1,0:T(8,128)(2,1)S(1)} %all-to-all-done.got_ref), custom_call_target="tpu_custom_call" | custom-call | tf_op jit(solution)/shard_map/select/pallas_call | solution.py:158
  26.7 3.3 %all-to-all-start.1 = ((bf16[4,128,128]{2,1,0:T(8,128)(2,1)}), bf16[4,128,128]{2,1,0:T(8,128)(2,1)S(1)}, u32[]{:S(2)}, u32[]{:S(2)}) async-start(bf16[4,128,128]{2,1,0:T(8,128)(2,1)} %select.1), calls=%async_computation.1 | async-start | bytes 262144 | tf_op jit(solution)/shard_map/all_to_all | solution.py:316
  30.0 0.0 collective-permute-done.2.refs_1_
  30.0 0.0 collective-permute-done.3.refs_2_
  30.1 0.2 collective-permute-done.4.refs_3_
  30.3 0.4 gram.1.sums_ref
  30.7 5.3 %all-to-all-done.1.held_ref = bf16[4,128,128]{2,1,0:T(8,128)(2,1)S(1)} async-done(((bf16[4,128,128]{2,1,0:T(8,128)(2,1)}), bf16[4,128,128]{2,1,0:T(8,128)(2,1)S(1)}, u32[]{:S(2)}, u32[]{:S(2)}) %all-to-all-start.1) | async-done | bytes 131104 | tf_op jit(solution)/shard_map/all_to_all | solution.py:316
  36.0 1.8 %precondition.1 = bf16[4,400,128]{2,1,0:T(8,128)(2,1)S(1)} custom-call(f32[3,256,256]{2,1,0:T(8,128)S(1)} %gram.1.sums_ref, bf16[4,128,128]{2,1,0:T(8,128)(2,1)S(1)} %all-to-all-done.1.held_ref), custom_call_target="tpu_custom_call" | custom-call | tf_op jit(solution)/shard_map/precondition/pallas_call | solution.py:305
  37.8 9.8 %all_to_all.15.got_ref = bf16[4,400,128]{2,1,0:T(8,128)(2,1)S(1)} all-to-all(bf16[4,400,128]{2,1,0:T(8,128)(2,1)S(1)} %precondition.1), channel_id=1, replica_groups=mesh['section'=16,'tensor'=8,'dp'=4] {'dp'}, dimensions={0} | all-to-all | bytes 819200 | tf_op jit(solution)/shard_map/all_to_all | solution.py:316
  47.7 1.1 %decode.1 = f32[12,128,128]{2,1,0:T(8,128)} custom-call(bf16[4,400,128]{2,1,0:T(8,128)(2,1)S(1)} %all_to_all.15.got_ref), custom_call_target="tpu_custom_call" | custom-call | tf_op jit(solution)/shard_map/decode/pallas_call | solution.py:253
Async XLA Ops:
  0.0 2.3 %copy-start.2 = (bf16[1,128,1536]{2,1,0:T(8,128)(2,1)S(1)}, bf16[1,128,1536]{2,1,0:T(8,128)(2,1)}, u32[]{:S(2)}) copy-start(bf16[1,128,1536]{2,1,0:T(8,128)(2,1)} %param.9) | copy-start | bytes 1179652
  0.0 5.2 %copy-start.3 = (bf16[1,128,1536]{2,1,0:T(8,128)(2,1)S(1)}, bf16[1,128,1536]{2,1,0:T(8,128)(2,1)}, u32[]{:S(2)}) copy-start(bf16[1,128,1536]{2,1,0:T(8,128)(2,1)} %param.7) | copy-start | bytes 1179652
  0.0 13.7 %copy-start.1 = (bf16[128,1536]{1,0:T(8,128)(2,1)S(1)}, bf16[128,1536]{1,0:T(8,128)(2,1)}, u32[]{:S(2)}) copy-start(bf16[128,1536]{1,0:T(8,128)(2,1)} %loss_ref.1) | copy-start | bytes 1179652
  2.3 11.4 %copy-start = (bf16[128,1536]{1,0:T(8,128)(2,1)S(1)}, bf16[128,1536]{1,0:T(8,128)(2,1)}, u32[]{:S(2)}) copy-start(bf16[128,1536]{1,0:T(8,128)(2,1)} %embedded_ref.1) | copy-start | bytes 1179652
  2.3 8.4 %collective-permute-start.1 = (bf16[128,1536]{1,0:T(8,128)(2,1)S(1)}, bf16[128,1536]{1,0:T(8,128)(2,1)S(1)}, u32[]{:S(2)}, u32[]{:S(2)}) collective-permute-start(bf16[128,1536]{1,0:T(8,128)(2,1)S(1)} %bitcast.8), channel_id=1, source_target_pairs={{0,480},{32,0},{64,32},{96,64},{128,96},{160,128},{192,160},{224,1... | collective-permute-start | bytes 1179656 | tf_op jit(solution)/shard_map/ppermute | solution.py:321
  5.2 8.4 %collective-permute-start = (bf16[128,1536]{1,0:T(8,128)(2,1)S(1)}, bf16[128,1536]{1,0:T(8,128)(2,1)S(1)}, u32[]{:S(2)}, u32[]{:S(2)}) collective-permute-start(bf16[128,1536]{1,0:T(8,128)(2,1)S(1)} %bitcast.9), channel_id=1, source_target_pairs={{0,32},{32,64},{64,96},{96,128},{128,160},{160,192},{192,224},{224... | collective-permute-start | bytes 1179656 | tf_op jit(solution)/shard_map/ppermute | solution.py:321
  5.2 20.7 %all-to-all-start = ((bf16[16,80,128]{2,1,0:T(8,128)(2,1)}), bf16[16,80,128]{2,1,0:T(8,128)(2,1)S(1)}, u32[]{:S(2)}, u32[]{:S(2)}) async-start(bf16[16,80,128]{2,1,0:T(8,128)(2,1)} %pack_state.1), calls=%async_computation | async-start | bytes 655360 | tf_op jit(solution)/shard_map/all_to_all | solution.py:316
  14.5 15.5 %collective-permute-start.2 = (bf16[2,128,384]{2,1,0:T(8,128)(2,1)S(1)}, bf16[2,128,384]{2,1,0:T(8,128)(2,1)S(1)}, u32[]{:S(2)}, u32[]{:S(2)}) collective-permute-start(bf16[2,128,384]{2,1,0:T(8,128)(2,1)S(1)} %get-tuple-element.14), channel_id=1, source_target_pairs={{0,1},{1,2},{2,3},{3,0},{4,5},{5,6},{6,7},{7,4},{8,9},{9,10},{10,1... | collective-permute-start | bytes 589832 | tf_op jit(solution)/shard_map/ppermute | solution.py:321
  17.9 12.1 %collective-permute-start.3 = (bf16[2,128,384]{2,1,0:T(8,128)(2,1)S(1)}, bf16[2,128,384]{2,1,0:T(8,128)(2,1)S(1)}, u32[]{:S(2)}, u32[]{:S(2)}) collective-permute-start(bf16[2,128,384]{2,1,0:T(8,128)(2,1)S(1)} %get-tuple-element.15), channel_id=1, source_target_pairs={{0,2},{1,3},{2,0},{3,1},{4,6},{5,7},{6,4},{7,5},{8,10},{9,11},{10,... | collective-permute-start | bytes 589832 | tf_op jit(solution)/shard_map/ppermute | solution.py:321
  22.5 7.7 %collective-permute-start.4 = (bf16[2,128,384]{2,1,0:T(8,128)(2,1)S(1)}, bf16[2,128,384]{2,1,0:T(8,128)(2,1)S(1)}, u32[]{:S(2)}, u32[]{:S(2)}) collective-permute-start(bf16[2,128,384]{2,1,0:T(8,128)(2,1)S(1)} %get-tuple-element.16), channel_id=1, source_target_pairs={{0,3},{1,0},{2,1},{3,2},{4,7},{5,4},{6,5},{7,6},{8,11},{9,8},{10,9... | collective-permute-start | bytes 589832 | tf_op jit(solution)/shard_map/ppermute | solution.py:321
  26.7 9.3 %all-to-all-start.1 = ((bf16[4,128,128]{2,1,0:T(8,128)(2,1)}), bf16[4,128,128]{2,1,0:T(8,128)(2,1)S(1)}, u32[]{:S(2)}, u32[]{:S(2)}) async-start(bf16[4,128,128]{2,1,0:T(8,128)(2,1)} %select.1), calls=%async_computation.1 | async-start | bytes 262144 | tf_op jit(solution)/shard_map/all_to_all | solution.py:316

commit v6 on v5

--- a/solution.py
+++ b/solution.py
@@ -329,7 +329,7 @@
     got = spread(packed, "section")
 
     *sends, slot = pack_tokens(assign[0, :, 0], arrived, embedded, returned, loss_grad)
-    chunks = [sends[0]] + [hop(sends[turn], "dp", turn) for turn in range(1, DP)]
+    chunks = [sends[0]] + [hop(sends[turn], "dp", turn) for turn in (2, 3, 1)]
 
     held = spread(select(slot, got), "dp")
 

time: 49.2 us -> 48.9 us (level)
    ppermute x5, waiting for transfers between devices: 3.12 us -> 4.46 us  [hop(): lax.ppermute(array, axis, [(i, (i + by) % size) for i in range(size)])]
    all_to_all x2, waiting for transfers between devices: 5.31 us -> 4.01 us  [spread(): return lax.all_to_all(array, axis, split_axis=0, concat_axis=0, tiled=True)]
    ppermute x5, starting transfers between devices: 14.3 us -> 13.7 us  [hop(): lax.ppermute(array, axis, [(i, (i + by) % size) for i in range(size)])]
where the time goes in v6:
time: 48.9 us; the launch traced here: 48.5 us
  starting transfers between devices  22.8 us (47%)
  blocking collectives  9.83 us (20%)
  waiting for transfers between devices  8.47 us (17%)
  Pallas kernels  7.22 us (15%)
    ppermute x5, starting transfers between devices, hop(): lax.ppermute(array, axis, [(i, (i + by) % size) for i in range(size)])  13.7 us
    all_to_all x1, blocking collectives, spread(): return lax.all_to_all(array, axis, split_axis=0, concat_axis=0, tiled=True)  9.83 us
    all_to_all x2, starting transfers between devices, spread(): return lax.all_to_all(array, axis, split_axis=0, concat_axis=0, tiled=True)  9.1 us
    ppermute x5, waiting for transfers between devices, hop(): lax.ppermute(array, axis, [(i, (i + by) % size) for i in range(size)])  4.46 us
    all_to_all x2, waiting for transfers between devices, spread(): return lax.all_to_all(array, axis, split_axis=0, concat_axis=0, tiled=True)  4.01 us
    pallas_call x1, Pallas kernels, pack_state(): pl.pallas_call(pack_state_kernel, out_shape=pltpu.VMEM((slots // 2, 2 * T...  2.28 us
    pallas_call x1, Pallas kernels, precondition(): pl.pallas_call(functools.partial(precondition_kernel, tokens_total), out_...  1.84 us
    pallas_call x1, Pallas kernels, decode(): pl.pallas_call(decode_kernel, out_shape=pltpu.HBM((blocks, BLK, BLK), jnp...  1.08 us
  transfers between devices with their start and end apart: 7, of which 3 were waited for; matrix products, arithmetic and copies ran while one was open for 0% of the time, Pallas kernels for 4%

profile of v6, /device:TPU:448, one launch (start us, length us, event | category | flops | bytes accessed | tf_op | source)
XLA Modules:
  0.0 48.5 jit_solution(5887406241895012959)
XLA Ops:
  0.0 0.0 copy-start.2
  0.0 0.0 copy-start.3
  0.0 0.0 copy-start.1
  0.0 2.3 %pack_state.1 = bf16[16,80,128]{2,1,0:T(8,128)(2,1)} custom-call(bf16[32,128,128]{2,1,0:T(8,128)(2,1)} %bitcast.6, bf16[32,128,128]{2,1,0:T(8,128)(2,1)} %bitcast.7), custom_call_target="tpu_custom_call" | custom-call | tf_op jit(solution)/shard_map/pack_state/pallas_call | solution.py:73
  2.3 0.0 copy-start
  2.3 0.0 copy-done.2
  2.3 2.9 %collective-permute-start.1 = (bf16[128,1536]{1,0:T(8,128)(2,1)S(1)}, bf16[128,1536]{1,0:T(8,128)(2,1)S(1)}, u32[]{:S(2)}, u32[]{:S(2)}) collective-permute-start(bf16[128,1536]{1,0:T(8,128)(2,1)S(1)} %bitcast.8), channel_id=1, source_target_pairs={{0,480},{32,0},{64,32},{96,64},{128,96},{160,128},{192,160},{224,1... | collective-permute-start | bytes 1179656 | tf_op jit(solution)/shard_map/ppermute | solution.py:321
  5.2 0.0 copy-done.3
  5.2 0.0 collective-permute-start
  5.2 5.5 %all-to-all-start = ((bf16[16,80,128]{2,1,0:T(8,128)(2,1)}), bf16[16,80,128]{2,1,0:T(8,128)(2,1)S(1)}, u32[]{:S(2)}, u32[]{:S(2)}) async-start(bf16[16,80,128]{2,1,0:T(8,128)(2,1)} %pack_state.1), calls=%async_computation | async-start | bytes 655360 | tf_op jit(solution)/shard_map/all_to_all | solution.py:316
  10.7 0.0 collective-permute-done.1.returned_ref
  10.7 2.9 %collective-permute-done.arrived_ref = bf16[128,1536]{1,0:T(8,128)(2,1)S(1)} collective-permute-done((bf16[128,1536]{1,0:T(8,128)(2,1)S(1)}, bf16[128,1536]{1,0:T(8,128)(2,1)S(1)}, u32[]{:S(2)}, u32[]{:S(2)}) %collective-permute-start) | collective-permute-done | bytes 393248 | tf_op jit(solution)/shard_map/ppermute | solution.py:321
  13.7 0.0 copy-done.1
  13.7 0.0 copy-done
  13.7 0.8 %pack_tokens.1 = (bf16[2,128,384]{2,1,0:T(8,128)(2,1)S(1)}, bf16[2,128,384]{2,1,0:T(8,128)(2,1)S(1)}, bf16[2,128,384]{2,1,0:T(8,128)(2,1)S(1)}, bf16[2,128,384]{2,1,0:T(8,128)(2,1)S(1)}, s32[12]{0:T(128)S(4)}) custom-call(s32[12]{0:T(128)} %bitcast.10, bf16[128,1536]{1,0:T(8,128)(2,1)S(1)} %collective-permute-done.arrived_ref, ...), custom_call_target="tpu_custom_call" | custom-call | flops 15000000512 | bytes 1048576 | tf_op jit(solution)/shard_map/pack_tokens/pallas_call | solution.py:122
  14.5 4.9 %collective-permute-start.2 = (bf16[2,128,384]{2,1,0:T(8,128)(2,1)S(1)}, bf16[2,128,384]{2,1,0:T(8,128)(2,1)S(1)}, u32[]{:S(2)}, u32[]{:S(2)}) collective-permute-start(bf16[2,128,384]{2,1,0:T(8,128)(2,1)S(1)} %get-tuple-element.14), channel_id=1, source_target_pairs={{0,2},{1,3},{2,0},{3,1},{4,6},{5,7},{6,4},{7,5},{8,10},{9,11},{10,... | collective-permute-start | bytes 589832 | tf_op jit(solution)/shard_map/ppermute | solution.py:321
  19.4 3.0 %collective-permute-start.3 = (bf16[2,128,384]{2,1,0:T(8,128)(2,1)S(1)}, bf16[2,128,384]{2,1,0:T(8,128)(2,1)S(1)}, u32[]{:S(2)}, u32[]{:S(2)}) collective-permute-start(bf16[2,128,384]{2,1,0:T(8,128)(2,1)S(1)} %get-tuple-element.15), channel_id=1, source_target_pairs={{0,3},{1,0},{2,1},{3,2},{4,7},{5,4},{6,5},{7,6},{8,11},{9,8},{10,9... | collective-permute-start | bytes 589832 | tf_op jit(solution)/shard_map/ppermute | solution.py:321
  22.5 2.8 %collective-permute-start.4 = (bf16[2,128,384]{2,1,0:T(8,128)(2,1)S(1)}, bf16[2,128,384]{2,1,0:T(8,128)(2,1)S(1)}, u32[]{:S(2)}, u32[]{:S(2)}) collective-permute-start(bf16[2,128,384]{2,1,0:T(8,128)(2,1)S(1)} %get-tuple-element.16), channel_id=1, source_target_pairs={{0,1},{1,2},{2,3},{3,0},{4,5},{5,6},{6,7},{7,4},{8,9},{9,10},{10,1... | collective-permute-start | bytes 589832 | tf_op jit(solution)/shard_map/ppermute | solution.py:321
  25.3 0.0 all-to-all-done.got_ref
  25.3 0.8 %select.1 = bf16[4,128,128]{2,1,0:T(8,128)(2,1)} custom-call(s32[12]{0:T(128)S(4)} %get-tuple-element.17.slot_ref, bf16[16,80,128]{2,1,0:T(8,128)(2,1)S(1)} %all-to-all-done.got_ref), custom_call_target="tpu_custom_call" | custom-call | tf_op jit(solution)/shard_map/select/pallas_call | solution.py:158
  26.1 3.6 %all-to-all-start.1 = ((bf16[4,128,128]{2,1,0:T(8,128)(2,1)}), bf16[4,128,128]{2,1,0:T(8,128)(2,1)S(1)}, u32[]{:S(2)}, u32[]{:S(2)}) async-start(bf16[4,128,128]{2,1,0:T(8,128)(2,1)} %select.1), calls=%async_computation.1 | async-start | bytes 262144 | tf_op jit(solution)/shard_map/all_to_all | solution.py:316
  29.7 0.0 collective-permute-done.2.refs_1_
  29.7 0.0 collective-permute-done.3.refs_2_
  29.7 1.5 %collective-permute-done.4.refs_3_ = bf16[2,128,384]{2,1,0:T(8,128)(2,1)S(1)} collective-permute-done((bf16[2,128,384]{2,1,0:T(8,128)(2,1)S(1)}, bf16[2,128,384]{2,1,0:T(8,128)(2,1)S(1)}, u32[]{:S(2)}, u32[]{:S(2)}) %collective-permute-start.4) | collective-permute-done | bytes 196640 | tf_op jit(solution)/shard_map/ppermute | solution.py:321
  31.3 0.4 gram.1.sums_ref
  31.7 4.0 %all-to-all-done.1.held_ref = bf16[4,128,128]{2,1,0:T(8,128)(2,1)S(1)} async-done(((bf16[4,128,128]{2,1,0:T(8,128)(2,1)}), bf16[4,128,128]{2,1,0:T(8,128)(2,1)S(1)}, u32[]{:S(2)}, u32[]{:S(2)}) %all-to-all-start.1) | async-done | bytes 131104 | tf_op jit(solution)/shard_map/all_to_all | solution.py:316
  35.7 1.8 %precondition.1 = bf16[4,400,128]{2,1,0:T(8,128)(2,1)S(1)} custom-call(f32[3,256,256]{2,1,0:T(8,128)S(1)} %gram.1.sums_ref, bf16[4,128,128]{2,1,0:T(8,128)(2,1)S(1)} %all-to-all-done.1.held_ref), custom_call_target="tpu_custom_call" | custom-call | tf_op jit(solution)/shard_map/precondition/pallas_call | solution.py:305
  37.5 9.8 %all_to_all.15.got_ref = bf16[4,400,128]{2,1,0:T(8,128)(2,1)S(1)} all-to-all(bf16[4,400,128]{2,1,0:T(8,128)(2,1)S(1)} %precondition.1), channel_id=1, replica_groups=mesh['section'=16,'tensor'=8,'dp'=4] {'dp'}, dimensions={0} | all-to-all | bytes 819200 | tf_op jit(solution)/shard_map/all_to_all | solution.py:316
  47.4 1.1 %decode.1 = f32[12,128,128]{2,1,0:T(8,128)} custom-call(bf16[4,400,128]{2,1,0:T(8,128)(2,1)S(1)} %all_to_all.15.got_ref), custom_call_target="tpu_custom_call" | custom-call | tf_op jit(solution)/shard_map/decode/pallas_call | solution.py:253
Async XLA Ops:
  0.0 2.3 %copy-start.2 = (bf16[1,128,1536]{2,1,0:T(8,128)(2,1)S(1)}, bf16[1,128,1536]{2,1,0:T(8,128)(2,1)}, u32[]{:S(2)}) copy-start(bf16[1,128,1536]{2,1,0:T(8,128)(2,1)} %param.9) | copy-start | bytes 1179652
  0.0 5.2 %copy-start.3 = (bf16[1,128,1536]{2,1,0:T(8,128)(2,1)S(1)}, bf16[1,128,1536]{2,1,0:T(8,128)(2,1)}, u32[]{:S(2)}) copy-start(bf16[1,128,1536]{2,1,0:T(8,128)(2,1)} %param.7) | copy-start | bytes 1179652
  0.0 13.7 %copy-start.1 = (bf16[128,1536]{1,0:T(8,128)(2,1)S(1)}, bf16[128,1536]{1,0:T(8,128)(2,1)}, u32[]{:S(2)}) copy-start(bf16[128,1536]{1,0:T(8,128)(2,1)} %loss_ref.1) | copy-start | bytes 1179652
  2.3 11.4 %copy-start = (bf16[128,1536]{1,0:T(8,128)(2,1)S(1)}, bf16[128,1536]{1,0:T(8,128)(2,1)}, u32[]{:S(2)}) copy-start(bf16[128,1536]{1,0:T(8,128)(2,1)} %embedded_ref.1) | copy-start | bytes 1179652
  2.3 8.4 %collective-permute-start.1 = (bf16[128,1536]{1,0:T(8,128)(2,1)S(1)}, bf16[128,1536]{1,0:T(8,128)(2,1)S(1)}, u32[]{:S(2)}, u32[]{:S(2)}) collective-permute-start(bf16[128,1536]{1,0:T(8,128)(2,1)S(1)} %bitcast.8), channel_id=1, source_target_pairs={{0,480},{32,0},{64,32},{96,64},{128,96},{160,128},{192,160},{224,1... | collective-permute-start | bytes 1179656 | tf_op jit(solution)/shard_map/ppermute | solution.py:321
  5.2 8.4 %collective-permute-start = (bf16[128,1536]{1,0:T(8,128)(2,1)S(1)}, bf16[128,1536]{1,0:T(8,128)(2,1)S(1)}, u32[]{:S(2)}, u32[]{:S(2)}) collective-permute-start(bf16[128,1536]{1,0:T(8,128)(2,1)S(1)} %bitcast.9), channel_id=1, source_target_pairs={{0,32},{32,64},{64,96},{96,128},{128,160},{160,192},{192,224},{224... | collective-permute-start | bytes 1179656 | tf_op jit(solution)/shard_map/ppermute | solution.py:321
  5.2 20.0 %all-to-all-start = ((bf16[16,80,128]{2,1,0:T(8,128)(2,1)}), bf16[16,80,128]{2,1,0:T(8,128)(2,1)S(1)}, u32[]{:S(2)}, u32[]{:S(2)}) async-start(bf16[16,80,128]{2,1,0:T(8,128)(2,1)} %pack_state.1), calls=%async_computation | async-start | bytes 655360 | tf_op jit(solution)/shard_map/all_to_all | solution.py:316
  14.5 15.2 %collective-permute-start.2 = (bf16[2,128,384]{2,1,0:T(8,128)(2,1)S(1)}, bf16[2,128,384]{2,1,0:T(8,128)(2,1)S(1)}, u32[]{:S(2)}, u32[]{:S(2)}) collective-permute-start(bf16[2,128,384]{2,1,0:T(8,128)(2,1)S(1)} %get-tuple-element.14), channel_id=1, source_target_pairs={{0,2},{1,3},{2,0},{3,1},{4,6},{5,7},{6,4},{7,5},{8,10},{9,11},{10,... | collective-permute-start | bytes 589832 | tf_op jit(solution)/shard_map/ppermute | solution.py:321
  19.4 10.3 %collective-permute-start.3 = (bf16[2,128,384]{2,1,0:T(8,128)(2,1)S(1)}, bf16[2,128,384]{2,1,0:T(8,128)(2,1)S(1)}, u32[]{:S(2)}, u32[]{:S(2)}) collective-permute-start(bf16[2,128,384]{2,1,0:T(8,128)(2,1)S(1)} %get-tuple-element.15), channel_id=1, source_target_pairs={{0,3},{1,0},{2,1},{3,2},{4,7},{5,4},{6,5},{7,6},{8,11},{9,8},{10,9... | collective-permute-start | bytes 589832 | tf_op jit(solution)/shard_map/ppermute | solution.py:321
  22.5 8.8 %collective-permute-start.4 = (bf16[2,128,384]{2,1,0:T(8,128)(2,1)S(1)}, bf16[2,128,384]{2,1,0:T(8,128)(2,1)S(1)}, u32[]{:S(2)}, u32[]{:S(2)}) collective-permute-start(bf16[2,128,384]{2,1,0:T(8,128)(2,1)S(1)} %get-tuple-element.16), channel_id=1, source_target_pairs={{0,1},{1,2},{2,3},{3,0},{4,5},{5,6},{6,7},{7,4},{8,9},{9,10},{10,1... | collective-permute-start | bytes 589832 | tf_op jit(solution)/shard_map/ppermute | solution.py:321
  26.1 9.6 %all-to-all-start.1 = ((bf16[4,128,128]{2,1,0:T(8,128)(2,1)}), bf16[4,128,128]{2,1,0:T(8,128)(2,1)S(1)}, u32[]{:S(2)}, u32[]{:S(2)}) async-start(bf16[4,128,128]{2,1,0:T(8,128)(2,1)} %select.1), calls=%async_computation.1 | async-start | bytes 262144 | tf_op jit(solution)/shard_map/all_to_all | solution.py:316

commit v7 on v6

--- a/solution.py
+++ b/solution.py
@@ -329,7 +329,7 @@
     got = spread(packed, "section")
 
     *sends, slot = pack_tokens(assign[0, :, 0], arrived, embedded, returned, loss_grad)
-    chunks = [sends[0]] + [hop(sends[turn], "dp", turn) for turn in (2, 3, 1)]
+    chunks = [sends[0]] + [hop(sends[turn], "dp", turn) for turn in (3, 2, 1)]
 
     held = spread(select(slot, got), "dp")
 

time: 48.9 us -> 49.2 us (level)
  the two profiles are of different devices: /device:TPU:448 before, /device:TPU:2 now
where the time goes in v7:
time: 49.2 us; the launch traced here: 48.8 us
  starting transfers between devices  24.6 us (50%)
  blocking collectives  9.83 us (20%)
  Pallas kernels  7.23 us (15%)
  waiting for transfers between devices  7.01 us (14%)
    ppermute x5, starting transfers between devices, hop(): lax.ppermute(array, axis, [(i, (i + by) % size) for i in range(size)])  13.4 us
    all_to_all x2, starting transfers between devices, spread(): return lax.all_to_all(array, axis, split_axis=0, concat_axis=0, tiled=True)  11.2 us
    all_to_all x1, blocking collectives, spread(): return lax.all_to_all(array, axis, split_axis=0, concat_axis=0, tiled=True)  9.83 us
    all_to_all x2, waiting for transfers between devices, spread(): return lax.all_to_all(array, axis, split_axis=0, concat_axis=0, tiled=True)  4.09 us
    ppermute x5, waiting for transfers between devices, hop(): lax.ppermute(array, axis, [(i, (i + by) % size) for i in range(size)])  2.92 us
    pallas_call x1, Pallas kernels, pack_state(): pl.pallas_call(pack_state_kernel, out_shape=pltpu.VMEM((slots // 2, 2 * T...  2.28 us
    pallas_call x1, Pallas kernels, precondition(): pl.pallas_call(functools.partial(precondition_kernel, tokens_total), out_...  1.85 us
    pallas_call x1, Pallas kernels, decode(): pl.pallas_call(decode_kernel, out_shape=pltpu.HBM((blocks, BLK, BLK), jnp...  1.08 us
  transfers between devices with their start and end apart: 7, of which 2 were waited for; matrix products, arithmetic and copies ran while one was open for 0% of the time, Pallas kernels for 4%

profile of v7, /device:TPU:2, one launch (start us, length us, event | category | flops | bytes accessed | tf_op | source)
XLA Modules:
  0.0 48.8 jit_solution(14978818689008144873)
XLA Ops:
  0.0 0.0 copy-start.2
  0.0 0.0 copy-start.3
  0.0 0.0 copy-start.1
  0.0 2.3 %pack_state.1 = bf16[16,80,128]{2,1,0:T(8,128)(2,1)} custom-call(bf16[32,128,128]{2,1,0:T(8,128)(2,1)} %bitcast.6, bf16[32,128,128]{2,1,0:T(8,128)(2,1)} %bitcast.7), custom_call_target="tpu_custom_call" | custom-call | tf_op jit(solution)/shard_map/pack_state/pallas_call | solution.py:73
  2.3 0.0 copy-start
  2.3 0.0 copy-done.2
  2.3 2.9 %collective-permute-start.1 = (bf16[128,1536]{1,0:T(8,128)(2,1)S(1)}, bf16[128,1536]{1,0:T(8,128)(2,1)S(1)}, u32[]{:S(2)}, u32[]{:S(2)}) collective-permute-start(bf16[128,1536]{1,0:T(8,128)(2,1)S(1)} %bitcast.8), channel_id=1, source_target_pairs={{0,480},{32,0},{64,32},{96,64},{128,96},{160,128},{192,160},{224,1... | collective-permute-start | bytes 1179656 | tf_op jit(solution)/shard_map/ppermute | solution.py:321
  5.2 0.0 copy-done.3
  5.2 0.0 collective-permute-start
  5.2 5.5 %all-to-all-start = ((bf16[16,80,128]{2,1,0:T(8,128)(2,1)}), bf16[16,80,128]{2,1,0:T(8,128)(2,1)S(1)}, u32[]{:S(2)}, u32[]{:S(2)}) async-start(bf16[16,80,128]{2,1,0:T(8,128)(2,1)} %pack_state.1), calls=%async_computation | async-start | bytes 655360 | tf_op jit(solution)/shard_map/all_to_all | solution.py:316
  10.7 0.0 collective-permute-done.1.returned_ref
  10.7 2.9 %collective-permute-done.arrived_ref = bf16[128,1536]{1,0:T(8,128)(2,1)S(1)} collective-permute-done((bf16[128,1536]{1,0:T(8,128)(2,1)S(1)}, bf16[128,1536]{1,0:T(8,128)(2,1)S(1)}, u32[]{:S(2)}, u32[]{:S(2)}) %collective-permute-start) | collective-permute-done | bytes 393248 | tf_op jit(solution)/shard_map/ppermute | solution.py:321
  13.7 0.0 copy-done.1
  13.7 0.0 copy-done
  13.7 0.8 %pack_tokens.1 = (bf16[2,128,384]{2,1,0:T(8,128)(2,1)S(1)}, bf16[2,128,384]{2,1,0:T(8,128)(2,1)S(1)}, bf16[2,128,384]{2,1,0:T(8,128)(2,1)S(1)}, bf16[2,128,384]{2,1,0:T(8,128)(2,1)S(1)}, s32[12]{0:T(128)S(4)}) custom-call(s32[12]{0:T(128)} %bitcast.10, bf16[128,1536]{1,0:T(8,128)(2,1)S(1)} %collective-permute-done.arrived_ref, ...), custom_call_target="tpu_custom_call" | custom-call | flops 15000000512 | bytes 1048576 | tf_op jit(solution)/shard_map/pack_tokens/pallas_call | solution.py:122
  14.5 4.9 %collective-permute-start.2 = (bf16[2,128,384]{2,1,0:T(8,128)(2,1)S(1)}, bf16[2,128,384]{2,1,0:T(8,128)(2,1)S(1)}, u32[]{:S(2)}, u32[]{:S(2)}) collective-permute-start(bf16[2,128,384]{2,1,0:T(8,128)(2,1)S(1)} %get-tuple-element.14), channel_id=1, source_target_pairs={{0,3},{1,0},{2,1},{3,2},{4,7},{5,4},{6,5},{7,6},{8,11},{9,8},{10,9... | collective-permute-start | bytes 589832 | tf_op jit(solution)/shard_map/ppermute | solution.py:321
  19.4 1.9 %collective-permute-start.3 = (bf16[2,128,384]{2,1,0:T(8,128)(2,1)S(1)}, bf16[2,128,384]{2,1,0:T(8,128)(2,1)S(1)}, u32[]{:S(2)}, u32[]{:S(2)}) collective-permute-start(bf16[2,128,384]{2,1,0:T(8,128)(2,1)S(1)} %get-tuple-element.15), channel_id=1, source_target_pairs={{0,2},{1,3},{2,0},{3,1},{4,6},{5,7},{6,4},{7,5},{8,10},{9,11},{10,... | collective-permute-start | bytes 589832 | tf_op jit(solution)/shard_map/ppermute | solution.py:321
  21.4 3.6 %collective-permute-start.4 = (bf16[2,128,384]{2,1,0:T(8,128)(2,1)S(1)}, bf16[2,128,384]{2,1,0:T(8,128)(2,1)S(1)}, u32[]{:S(2)}, u32[]{:S(2)}) collective-permute-start(bf16[2,128,384]{2,1,0:T(8,128)(2,1)S(1)} %get-tuple-element.16), channel_id=1, source_target_pairs={{0,1},{1,2},{2,3},{3,0},{4,5},{5,6},{6,7},{7,4},{8,9},{9,10},{10,1... | collective-permute-start | bytes 589832 | tf_op jit(solution)/shard_map/ppermute | solution.py:321
  25.0 0.0 all-to-all-done.got_ref
  25.0 0.8 %select.1 = bf16[4,128,128]{2,1,0:T(8,128)(2,1)} custom-call(s32[12]{0:T(128)S(4)} %get-tuple-element.17.slot_ref, bf16[16,80,128]{2,1,0:T(8,128)(2,1)S(1)} %all-to-all-done.got_ref), custom_call_target="tpu_custom_call" | custom-call | tf_op jit(solution)/shard_map/select/pallas_call | solution.py:158
  25.8 5.7 %all-to-all-start.1 = ((bf16[4,128,128]{2,1,0:T(8,128)(2,1)}), bf16[4,128,128]{2,1,0:T(8,128)(2,1)S(1)}, u32[]{:S(2)}, u32[]{:S(2)}) async-start(bf16[4,128,128]{2,1,0:T(8,128)(2,1)} %select.1), calls=%async_computation.1 | async-start | bytes 262144 | tf_op jit(solution)/shard_map/all_to_all | solution.py:316
  31.5 0.0 collective-permute-done.2.refs_1_
  31.5 0.0 collective-permute-done.3.refs_2_
  31.5 0.0 collective-permute-done.4.refs_3_
  31.5 0.4 gram.1.sums_ref
  31.9 4.1 %all-to-all-done.1.held_ref = bf16[4,128,128]{2,1,0:T(8,128)(2,1)S(1)} async-done(((bf16[4,128,128]{2,1,0:T(8,128)(2,1)}), bf16[4,128,128]{2,1,0:T(8,128)(2,1)S(1)}, u32[]{:S(2)}, u32[]{:S(2)}) %all-to-all-start.1) | async-done | bytes 131104 | tf_op jit(solution)/shard_map/all_to_all | solution.py:316
  36.0 1.8 %precondition.1 = bf16[4,400,128]{2,1,0:T(8,128)(2,1)S(1)} custom-call(f32[3,256,256]{2,1,0:T(8,128)S(1)} %gram.1.sums_ref, bf16[4,128,128]{2,1,0:T(8,128)(2,1)S(1)} %all-to-all-done.1.held_ref), custom_call_target="tpu_custom_call" | custom-call | tf_op jit(solution)/shard_map/precondition/pallas_call | solution.py:305
  37.9 9.8 %all_to_all.15.got_ref = bf16[4,400,128]{2,1,0:T(8,128)(2,1)S(1)} all-to-all(bf16[4,400,128]{2,1,0:T(8,128)(2,1)S(1)} %precondition.1), channel_id=1, replica_groups=mesh['section'=16,'tensor'=8,'dp'=4] {'dp'}, dimensions={0} | all-to-all | bytes 819200 | tf_op jit(solution)/shard_map/all_to_all | solution.py:316
  47.7 1.1 %decode.1 = f32[12,128,128]{2,1,0:T(8,128)} custom-call(bf16[4,400,128]{2,1,0:T(8,128)(2,1)S(1)} %all_to_all.15.got_ref), custom_call_target="tpu_custom_call" | custom-call | tf_op jit(solution)/shard_map/decode/pallas_call | solution.py:253
Async XLA Ops:
  0.0 2.3 %copy-start.2 = (bf16[1,128,1536]{2,1,0:T(8,128)(2,1)S(1)}, bf16[1,128,1536]{2,1,0:T(8,128)(2,1)}, u32[]{:S(2)}) copy-start(bf16[1,128,1536]{2,1,0:T(8,128)(2,1)} %param.9) | copy-start | bytes 1179652
  0.0 5.2 %copy-start.3 = (bf16[1,128,1536]{2,1,0:T(8,128)(2,1)S(1)}, bf16[1,128,1536]{2,1,0:T(8,128)(2,1)}, u32[]{:S(2)}) copy-start(bf16[1,128,1536]{2,1,0:T(8,128)(2,1)} %param.7) | copy-start | bytes 1179652
  0.0 13.7 %copy-start.1 = (bf16[128,1536]{1,0:T(8,128)(2,1)S(1)}, bf16[128,1536]{1,0:T(8,128)(2,1)}, u32[]{:S(2)}) copy-start(bf16[128,1536]{1,0:T(8,128)(2,1)} %loss_ref.1) | copy-start | bytes 1179652
  2.3 11.4 %copy-start = (bf16[128,1536]{1,0:T(8,128)(2,1)S(1)}, bf16[128,1536]{1,0:T(8,128)(2,1)}, u32[]{:S(2)}) copy-start(bf16[128,1536]{1,0:T(8,128)(2,1)} %embedded_ref.1) | copy-start | bytes 1179652
  2.3 8.4 %collective-permute-start.1 = (bf16[128,1536]{1,0:T(8,128)(2,1)S(1)}, bf16[128,1536]{1,0:T(8,128)(2,1)S(1)}, u32[]{:S(2)}, u32[]{:S(2)}) collective-permute-start(bf16[128,1536]{1,0:T(8,128)(2,1)S(1)} %bitcast.8), channel_id=1, source_target_pairs={{0,480},{32,0},{64,32},{96,64},{128,96},{160,128},{192,160},{224,1... | collective-permute-start | bytes 1179656 | tf_op jit(solution)/shard_map/ppermute | solution.py:321
  5.2 8.4 %collective-permute-start = (bf16[128,1536]{1,0:T(8,128)(2,1)S(1)}, bf16[128,1536]{1,0:T(8,128)(2,1)S(1)}, u32[]{:S(2)}, u32[]{:S(2)}) collective-permute-start(bf16[128,1536]{1,0:T(8,128)(2,1)S(1)} %bitcast.9), channel_id=1, source_target_pairs={{0,32},{32,64},{64,96},{96,128},{128,160},{160,192},{192,224},{224... | collective-permute-start | bytes 1179656 | tf_op jit(solution)/shard_map/ppermute | solution.py:321
  5.2 19.8 %all-to-all-start = ((bf16[16,80,128]{2,1,0:T(8,128)(2,1)}), bf16[16,80,128]{2,1,0:T(8,128)(2,1)S(1)}, u32[]{:S(2)}, u32[]{:S(2)}) async-start(bf16[16,80,128]{2,1,0:T(8,128)(2,1)} %pack_state.1), calls=%async_computation | async-start | bytes 655360 | tf_op jit(solution)/shard_map/all_to_all | solution.py:316
  14.5 17.0 %collective-permute-start.2 = (bf16[2,128,384]{2,1,0:T(8,128)(2,1)S(1)}, bf16[2,128,384]{2,1,0:T(8,128)(2,1)S(1)}, u32[]{:S(2)}, u32[]{:S(2)}) collective-permute-start(bf16[2,128,384]{2,1,0:T(8,128)(2,1)S(1)} %get-tuple-element.14), channel_id=1, source_target_pairs={{0,3},{1,0},{2,1},{3,2},{4,7},{5,4},{6,5},{7,6},{8,11},{9,8},{10,9... | collective-permute-start | bytes 589832 | tf_op jit(solution)/shard_map/ppermute | solution.py:321
  19.4 12.1 %collective-permute-start.3 = (bf16[2,128,384]{2,1,0:T(8,128)(2,1)S(1)}, bf16[2,128,384]{2,1,0:T(8,128)(2,1)S(1)}, u32[]{:S(2)}, u32[]{:S(2)}) collective-permute-start(bf16[2,128,384]{2,1,0:T(8,128)(2,1)S(1)} %get-tuple-element.15), channel_id=1, source_target_pairs={{0,2},{1,3},{2,0},{3,1},{4,6},{5,7},{6,4},{7,5},{8,10},{9,11},{10,... | collective-permute-start | bytes 589832 | tf_op jit(solution)/shard_map/ppermute | solution.py:321
  21.4 10.1 %collective-permute-start.4 = (bf16[2,128,384]{2,1,0:T(8,128)(2,1)S(1)}, bf16[2,128,384]{2,1,0:T(8,128)(2,1)S(1)}, u32[]{:S(2)}, u32[]{:S(2)}) collective-permute-start(bf16[2,128,384]{2,1,0:T(8,128)(2,1)S(1)} %get-tuple-element.16), channel_id=1, source_target_pairs={{0,1},{1,2},{2,3},{3,0},{4,5},{5,6},{6,7},{7,4},{8,9},{9,10},{10,1... | collective-permute-start | bytes 589832 | tf_op jit(solution)/shard_map/ppermute | solution.py:321
  25.8 10.2 %all-to-all-start.1 = ((bf16[4,128,128]{2,1,0:T(8,128)(2,1)}), bf16[4,128,128]{2,1,0:T(8,128)(2,1)S(1)}, u32[]{:S(2)}, u32[]{:S(2)}) async-start(bf16[4,128,128]{2,1,0:T(8,128)(2,1)} %select.1), calls=%async_computation.1 | async-start | bytes 262144 | tf_op jit(solution)/shard_map/all_to_all | solution.py:316
